TPU v7x, 32 devices: a whole 2x2x4 slice. The times are simulated.
32 devices in a mesh: sta: 8 (over y, x, core), tm: 4 (over z).
Axes of the slice: x: 2, y: 2, z: 4, core: 2. Of those that a mesh axis runs over, the one named last changes fastest.
Arguments:
- records: bfloat16 [1024, 1024], P('sta', 'tm'), may hold values from -6 to 6
- filter_taps: float32 [127], replicated, may hold values from -0.5 to 0.5
- plan: int32 [3], replicated, may hold values from 1 to 7, as said below
- station_valid: int32 [1024], P('sta'), may hold values 0 or 1
Outputs:
- correlations: bfloat16 [3, 1024, 101, 128], P(None, ('sta', 'tm'))
Inputs may be any that keep to these rules, and one draw needn't show every extreme that they name: `plan`: the 3 distances are distinct, and one of them is 7.
All inputs are finite; a program needn't handle non-finite values. No bound on the sum of `station_valid` on one device may be relied on, other than what follows from the above.
Results may differ from a plain program's by a relative error of at most 0.0048.
Values may be sent and summed in bfloat16 or wider, within the bound.
A program may use at most 64 MiB of HBM per device.

v0:
```python
import jax
import jax.numpy as jnp
from jax import lax
from jax.sharding import PartitionSpec as P

AVG_HALF = 64
LAGS = 101
ROUNDS = 3


tile_len = 128


def partner_2(value, axis, bit):
    mask = 2**bit
    pairs = [(source, source ^ mask) for source in range(lax.axis_size(axis))]
    return lax.ppermute(value, axis, pairs)


def extended_2(array, sides, width):
    for axis, dim in sides:
        devices, length = (lax.axis_size(axis), array.shape[dim])
        up = [(i, (i + 1) % devices) for i in range(devices - 1)]
        down = [(j, i) for i, j in up]
        last = lax.slice_in_dim(array, length - width, length, axis=dim)
        initial = lax.slice_in_dim(array, 0, width, axis=dim)
        before = lax.ppermute(last, axis, up)
        after = lax.ppermute(initial, axis, down)
        array = jnp.concatenate([before, array, after], axis=dim)
    return array


def banded(coeffs, out_rows):
    tap_count = coeffs.shape[0]
    span_len = out_rows + tap_count - 1
    padded = jnp.concatenate([coeffs, jnp.zeros((span_len + 1 - tap_count,), coeffs.dtype)])
    flattened = jnp.tile(padded, out_rows)[: out_rows * span_len]
    return flattened.reshape(out_rows, span_len)


def apply_band(extended, matrix):
    return lax.dot_general(
        extended,
        matrix,
        (((1,), (1,)), ((), ())),
        precision=lax.Precision.HIGHEST,
        preferred_element_type=jnp.float32,
    )


def correlate(own_rows, partner, lag_count):
    n = own_rows.shape[0]
    total_len = own_rows.shape[1]
    half_lags = (lag_count - 1) // 2
    span_len = tile_len + lag_count - 1
    padded = jnp.pad(partner, ((0, 0), (half_lags, half_lags)))

    def tile_step(index, carried):
        offset = index * tile_len
        block_rows = lax.dynamic_slice_in_dim(own_rows, offset, tile_len, 1)
        extended = jnp.concatenate(
            [block_rows, jnp.zeros((n, lag_count), block_rows.dtype)], axis=1
        )
        toeplitz = jnp.tile(extended, (1, lag_count))[:, : lag_count * span_len].reshape(
            n, lag_count, span_len
        )
        window = lax.dynamic_slice_in_dim(padded, offset, span_len, 1)
        return carried + jnp.einsum(
            "ilw,jw->ilj", toeplitz, window, preferred_element_type=jnp.float32
        )

    zeros_init = jnp.zeros((n, lag_count, partner.shape[0]), jnp.float32)
    return lax.fori_loop(0, total_len // tile_len, tile_step, zeros_init)


def bit_order(bit_count):
    return list(range(bit_count))


def route_whole(start, plan, bit_count):
    routed_list = []
    for r in range(ROUNDS):
        distance = plan[r]
        routed = start
        for b in bit_order(bit_count):
            arrived = partner_2(routed, "sta", b)
            routed = jnp.where(distance // 2**b % 2 == 1, arrived, routed)
        routed_list.append(routed)
    return routed_list


def local(records, filter_taps, plan, station_valid):
    samp_dev = records.shape[1]
    half_taps = (filter_taps.shape[0] - 1) // 2
    half_avg = AVG_HALF
    tm_index = lax.axis_index("tm")
    box_taps = jnp.full((2 * half_avg + 1,), 1.0 / (2 * half_avg + 1), jnp.float32)
    raw_ext = extended_2(records, (("tm", 1),), half_taps + half_avg)
    wide_len = samp_dev + 2 * half_avg
    filt_ext = apply_band(raw_ext.astype(jnp.float32), banded(filter_taps, wide_len))
    positions = tm_index * samp_dev - half_avg + jnp.arange(wide_len, dtype=jnp.int32)
    inside = (positions >= 0) & (positions < samp_dev * lax.axis_size("tm"))
    filt_ext = jnp.where(inside[None, :], filt_ext, 0.0)
    filtered = filt_ext[:, half_avg : half_avg + samp_dev]
    magnitude = apply_band(jnp.abs(filt_ext), banded(box_taps, samp_dev)) + 1e-05
    normalized = (filtered / magnitude * station_valid[:, None].astype(jnp.float32)).astype(
        jnp.bfloat16
    )
    my_rows = lax.all_to_all(normalized, "tm", split_axis=0, concat_axis=1, tiled=True)
    lag_count = LAGS
    bit_count = lax.axis_size("sta").bit_length() - 1
    factor = 1.0 / jnp.sqrt(jnp.float32(my_rows.shape[1]))
    results = []
    whole_block = lax.all_gather(my_rows, "tm", axis=0, tiled=True)
    for routed in route_whole(whole_block, plan, bit_count):
        results.append(correlate(my_rows, routed, lag_count))
    return (jnp.stack(results) * factor).astype(jnp.bfloat16)


def solution(mesh):
    return jax.shard_map(
        local,
        mesh=mesh,
        in_specs=(P("sta", "tm"), P(), P(), P("sta")),
        out_specs=P(None, ("sta", "tm"), None, None),
        check_vma=False,
    )
```

profile of v0, /device:TPU:0, one launch (start us, length us, event | category | flops | bytes accessed | tf_op | source)
XLA Modules:
  0.0 326.0 jit_solution(8728676778431697167)
XLA Ops:
  0.9 4.9 %collective-permute-start = (bf16[128,127]{1,0:T(8,128)(2,1)S(1)}, bf16[128,127]{1,0:T(8,128)(2,1)S(1)}, u32[]{:S(2)}, u32[]{:S(2)}) collective-permute-start(bf16[128,127]{1,0:T(8,128)(2,1)S(1)} %get-tuple-element.329), channel_id=1, source_target_pairs={{0,1},{1,2},{2,3},{4,5},{5,6},{6,7},{8,9},{9,10},{10,11},{12,13},{... | collective-permute-start | bytes 97544 | tf_op jit(solution)/shard_map/ppermute | solution.py:27
  12.7 10.6 %all_to_all.19 = bf16[4,32,256]{2,1,0:T(8,128)(2,1)S(1)} all-to-all(bf16[4,32,256]{2,1,0:T(8,128)(2,1)S(1)} %bitcast.46), channel_id=1, replica_groups=mesh['sta'=8,'tm'=4] {'tm'}, dimensions={0} | all-to-all | bytes 131072 | tf_op jit(solution)/shard_map/all_to_all | solution.py:109
  23.3 13.8 %all_gather.3 = bf16[128,1024]{1,0:T(8,128)(2,1)S(1)} all-gather(bf16[32,1024]{1,0:T(8,128)(2,1)S(1)} %bitcast.43), channel_id=1, replica_groups=mesh['sta'=8,'tm'=4] {'tm'}, dimensions={0}, use_global_device_ids=true | all-gather | bytes 327680 | tf_op jit(solution)/shard_map/all_gather | solution.py:114
  72.7 82.3 %while.44 = (s32[]{:T(128)}, f32[32,101,128]{2,1,0:T(8,128)}, bf16[32,1024]{1,0:T(8,128)(2,1)S(1)}, bf16[128,1124]{0,1:T(8,128)(2,1)}, s32[]{:T(128)}, /*index=5...) while((s32[]{:T(128)}, f32[32,101,128]{2,1,0:T(8,128)}, bf16[32,1024]{1,0:T(8,128)(2,1)S(1)}, ...), condition=%wide.region_5.6_spmd.clone, body=%wide.region_4.5_spmd.clone.sunk | while | flops 189472768 | bytes 28471100 | solution.py:73
  75.7 4.4 %reshape.65 = bf16[32,101,228]{2,1,0:T(8,128)(2,1)S(1)} reshape(bf16[32,23028]{1,0:T(8,128)(2,1)} %slice.77) | data formatting | bytes 2947584 | tf_op jit(solution)/shard_map/while/body/eval_jaxpr/reshape | solution.py:64
  86.0 4.4 %reshape.65 = bf16[32,101,228]{2,1,0:T(8,128)(2,1)S(1)} reshape(bf16[32,23028]{1,0:T(8,128)(2,1)} %slice.77) | data formatting | bytes 2947584 | tf_op jit(solution)/shard_map/while/body/eval_jaxpr/reshape | solution.py:64
  96.3 4.4 %reshape.65 = bf16[32,101,228]{2,1,0:T(8,128)(2,1)S(1)} reshape(bf16[32,23028]{1,0:T(8,128)(2,1)} %slice.77) | data formatting | bytes 2947584 | tf_op jit(solution)/shard_map/while/body/eval_jaxpr/reshape | solution.py:64
  106.6 4.4 %reshape.65 = bf16[32,101,228]{2,1,0:T(8,128)(2,1)S(1)} reshape(bf16[32,23028]{1,0:T(8,128)(2,1)} %slice.77) | data formatting | bytes 2947584 | tf_op jit(solution)/shard_map/while/body/eval_jaxpr/reshape | solution.py:64
  116.8 4.4 %reshape.65 = bf16[32,101,228]{2,1,0:T(8,128)(2,1)S(1)} reshape(bf16[32,23028]{1,0:T(8,128)(2,1)} %slice.77) | data formatting | bytes 2947584 | tf_op jit(solution)/shard_map/while/body/eval_jaxpr/reshape | solution.py:64
  127.1 4.4 %reshape.65 = bf16[32,101,228]{2,1,0:T(8,128)(2,1)S(1)} reshape(bf16[32,23028]{1,0:T(8,128)(2,1)} %slice.77) | data formatting | bytes 2947584 | tf_op jit(solution)/shard_map/while/body/eval_jaxpr/reshape | solution.py:64
  137.4 4.4 %reshape.65 = bf16[32,101,228]{2,1,0:T(8,128)(2,1)S(1)} reshape(bf16[32,23028]{1,0:T(8,128)(2,1)} %slice.77) | data formatting | bytes 2947584 | tf_op jit(solution)/shard_map/while/body/eval_jaxpr/reshape | solution.py:64
  147.7 4.4 %reshape.65 = bf16[32,101,228]{2,1,0:T(8,128)(2,1)S(1)} reshape(bf16[32,23028]{1,0:T(8,128)(2,1)} %slice.77) | data formatting | bytes 2947584 | tf_op jit(solution)/shard_map/while/body/eval_jaxpr/reshape | solution.py:64
  155.0 82.3 %while.43 = (s32[]{:T(128)}, f32[32,101,128]{2,1,0:T(8,128)}, bf16[32,1024]{1,0:T(8,128)(2,1)S(1)}, bf16[128,1124]{0,1:T(8,128)(2,1)}, s32[]{:T(128)}, /*index=5...) while((s32[]{:T(128)}, f32[32,101,128]{2,1,0:T(8,128)}, bf16[32,1024]{1,0:T(8,128)(2,1)S(1)}, ...), condition=%wide.region_3.4_spmd.clone, body=%wide.region_2.3_spmd.clone.sunk | while | flops 189472768 | bytes 28471100 | solution.py:73
  158.0 4.4 %reshape.64 = bf16[32,101,228]{2,1,0:T(8,128)(2,1)S(1)} reshape(bf16[32,23028]{1,0:T(8,128)(2,1)} %slice.76) | data formatting | bytes 2947584 | tf_op jit(solution)/shard_map/while/body/eval_jaxpr/reshape | solution.py:64
  168.3 4.4 %reshape.64 = bf16[32,101,228]{2,1,0:T(8,128)(2,1)S(1)} reshape(bf16[32,23028]{1,0:T(8,128)(2,1)} %slice.76) | data formatting | bytes 2947584 | tf_op jit(solution)/shard_map/while/body/eval_jaxpr/reshape | solution.py:64
  178.6 4.4 %reshape.64 = bf16[32,101,228]{2,1,0:T(8,128)(2,1)S(1)} reshape(bf16[32,23028]{1,0:T(8,128)(2,1)} %slice.76) | data formatting | bytes 2947584 | tf_op jit(solution)/shard_map/while/body/eval_jaxpr/reshape | solution.py:64
  188.8 4.4 %reshape.64 = bf16[32,101,228]{2,1,0:T(8,128)(2,1)S(1)} reshape(bf16[32,23028]{1,0:T(8,128)(2,1)} %slice.76) | data formatting | bytes 2947584 | tf_op jit(solution)/shard_map/while/body/eval_jaxpr/reshape | solution.py:64
  199.1 4.4 %reshape.64 = bf16[32,101,228]{2,1,0:T(8,128)(2,1)S(1)} reshape(bf16[32,23028]{1,0:T(8,128)(2,1)} %slice.76) | data formatting | bytes 2947584 | tf_op jit(solution)/shard_map/while/body/eval_jaxpr/reshape | solution.py:64
  209.4 4.4 %reshape.64 = bf16[32,101,228]{2,1,0:T(8,128)(2,1)S(1)} reshape(bf16[32,23028]{1,0:T(8,128)(2,1)} %slice.76) | data formatting | bytes 2947584 | tf_op jit(solution)/shard_map/while/body/eval_jaxpr/reshape | solution.py:64
  219.7 4.4 %reshape.64 = bf16[32,101,228]{2,1,0:T(8,128)(2,1)S(1)} reshape(bf16[32,23028]{1,0:T(8,128)(2,1)} %slice.76) | data formatting | bytes 2947584 | tf_op jit(solution)/shard_map/while/body/eval_jaxpr/reshape | solution.py:64
  237.3 82.6 %while.42 = (s32[]{:T(128)}, f32[32,101,128]{2,1,0:T(8,128)}, bf16[32,1024]{1,0:T(8,128)(2,1)S(1)}, bf16[128,1124]{0,1:T(8,128)(2,1)}, s32[]{:T(128)}, /*index=5...) while((s32[]{:T(128)}, f32[32,101,128]{2,1,0:T(8,128)}, bf16[32,1024]{1,0:T(8,128)(2,1)S(1)}, ...), condition=%wide.region_1.2_spmd.clone, body=%wide.region_0.1_spmd.clone.sunk | while | flops 189472768 | bytes 28471100 | solution.py:73
  240.3 4.4 %reshape.63 = bf16[32,101,228]{2,1,0:T(8,128)(2,1)S(1)} reshape(bf16[32,23028]{1,0:T(8,128)(2,1)} %slice.75) | data formatting | bytes 2947584 | tf_op jit(solution)/shard_map/while/body/eval_jaxpr/reshape | solution.py:64
  281.6 4.4 %reshape.63 = bf16[32,101,228]{2,1,0:T(8,128)(2,1)S(1)} reshape(bf16[32,23028]{1,0:T(8,128)(2,1)} %slice.75) | data formatting | bytes 2947584 | tf_op jit(solution)/shard_map/while/body/eval_jaxpr/reshape | solution.py:64
  291.9 4.4 %reshape.63 = bf16[32,101,228]{2,1,0:T(8,128)(2,1)S(1)} reshape(bf16[32,23028]{1,0:T(8,128)(2,1)} %slice.75) | data formatting | bytes 2947584 | tf_op jit(solution)/shard_map/while/body/eval_jaxpr/reshape | solution.py:64
  (305 shorter events, 208.2 us)
Async XLA Ops:
  0.0 9.1 %copy-start.9 = (f32[127]{0:T(128)S(1)}, f32[127]{0:T(128)}, u32[]{:S(2)}) copy-start(f32[127]{0:T(128)} %param.11) | copy-start | bytes 1528
  0.9 9.9 %collective-permute-start = (bf16[128,127]{1,0:T(8,128)(2,1)S(1)}, bf16[128,127]{1,0:T(8,128)(2,1)S(1)}, u32[]{:S(2)}, u32[]{:S(2)}) collective-permute-start(bf16[128,127]{1,0:T(8,128)(2,1)S(1)} %get-tuple-element.329), channel_id=1, source_target_pairs={{0,1},{1,2},{2,3},{4,5},{5,6},{6,7},{8,9},{9,10},{10,11},{12,13},{... | collective-permute-start | bytes 97544 | tf_op jit(solution)/shard_map/ppermute | solution.py:27
  5.8 5.8 %collective-permute-start.1 = (bf16[128,127]{1,0:T(8,128)(2,1)S(1)}, bf16[128,127]{1,0:T(8,128)(2,1)S(1)}, u32[]{:S(2)}, u32[]{:S(2)}) collective-permute-start(bf16[128,127]{1,0:T(8,128)(2,1)S(1)} %get-tuple-element.330), channel_id=1, source_target_pairs={{1,0},{2,1},{3,2},{5,4},{6,5},{7,6},{9,8},{10,9},{11,10},{13,12},{... | collective-permute-start | bytes 97544 | tf_op jit(solution)/shard_map/ppermute | solution.py:28
  10.1 27.0 %copy-start.8 = (s32[3]{0:T(128)S(1)}, s32[3]{0:T(128)}, u32[]{:S(2)}) copy-start(s32[3]{0:T(128)} %param.12) | copy-start | bytes 40
  37.1 6.4 %collective-permute-start.2 = (bf16[128,1024]{1,0:T(8,128)(2,1)S(1)}, bf16[128,1024]{1,0:T(8,128)(2,1)S(1)}, u32[]{:S(2)}, u32[]{:S(2)}) collective-permute-start(bf16[128,1024]{1,0:T(8,128)(2,1)S(1)} %all_gather.3), channel_id=1, source_target_pairs={{0,4},{4,0},{8,12},{12,8},{16,20},{20,16},{24,28},{28,24},{1,5},{5... | collective-permute-start | bytes 786440 | tf_op jit(solution)/shard_map/ppermute | solution.py:17
  43.7 9.2 %collective-permute-start.3 = (bf16[128,1024]{1,0:T(8,128)(2,1)S(1)}, bf16[128,1024]{1,0:T(8,128)(2,1)S(1)}, u32[]{:S(2)}, u32[]{:S(2)}) collective-permute-start(bf16[128,1024]{1,0:T(8,128)(2,1)S(1)} %get-tuple-element.326), channel_id=1, source_target_pairs={{0,8},{4,12},{8,0},{12,4},{16,24},{20,28},{24,16},{28,20},{1,9},{5... | collective-permute-start | bytes 786440 | tf_op jit(solution)/shard_map/ppermute | solution.py:17
  45.2 13.2 %collective-permute-start.7 = (bf16[128,1024]{1,0:T(8,128)(2,1)S(1)}, bf16[128,1024]{1,0:T(8,128)(2,1)S(1)}, u32[]{:S(2)}, u32[]{:S(2)}) collective-permute-start(bf16[128,1024]{1,0:T(8,128)(2,1)S(1)} %get-tuple-element.327), channel_id=1, source_target_pairs={{0,8},{4,12},{8,0},{12,4},{16,24},{20,28},{24,16},{28,20},{1,9},{5... | collective-permute-start | bytes 786440 | tf_op jit(solution)/shard_map/ppermute | solution.py:17
  47.9 15.7 %collective-permute-start.5 = (bf16[128,1024]{1,0:T(8,128)(2,1)S(1)}, bf16[128,1024]{1,0:T(8,128)(2,1)S(1)}, u32[]{:S(2)}, u32[]{:S(2)}) collective-permute-start(bf16[128,1024]{1,0:T(8,128)(2,1)S(1)} %get-tuple-element.328), channel_id=1, source_target_pairs={{0,8},{4,12},{8,0},{12,4},{16,24},{20,28},{24,16},{28,20},{1,9},{5... | collective-permute-start | bytes 786440 | tf_op jit(solution)/shard_map/ppermute | solution.py:17
  52.9 12.4 %collective-permute-start.4 = (bf16[128,1024]{1,0:T(8,128)(2,1)S(1)}, bf16[128,1024]{1,0:T(8,128)(2,1)S(1)}, u32[]{:S(2)}, u32[]{:S(2)}) collective-permute-start(bf16[128,1024]{1,0:T(8,128)(2,1)S(1)} %broadcast_select_fusion.7), channel_id=1, source_target_pairs={{0,16},{4,20},{8,24},{12,28},{16,0},{20,4},{24,8},{28,12},{1,17},{... | collective-permute-start | bytes 786440 | tf_op jit(solution)/shard_map/ppermute | solution.py:17
  58.5 7.6 %collective-permute-start.8 = (bf16[128,1024]{1,0:T(8,128)(2,1)S(1)}, bf16[128,1024]{1,0:T(8,128)(2,1)S(1)}, u32[]{:S(2)}, u32[]{:S(2)}) collective-permute-start(bf16[128,1024]{1,0:T(8,128)(2,1)S(1)} %broadcast_select_fusion.1), channel_id=1, source_target_pairs={{0,16},{4,20},{8,24},{12,28},{16,0},{20,4},{24,8},{28,12},{1,17},{... | collective-permute-start | bytes 786440 | tf_op jit(solution)/shard_map/ppermute | solution.py:17
  63.7 8.0 %collective-permute-start.6 = (bf16[128,1024]{1,0:T(8,128)(2,1)S(1)}, bf16[128,1024]{1,0:T(8,128)(2,1)S(1)}, u32[]{:S(2)}, u32[]{:S(2)}) collective-permute-start(bf16[128,1024]{1,0:T(8,128)(2,1)S(1)} %broadcast_select_fusion.4), channel_id=1, source_target_pairs={{0,16},{4,20},{8,24},{12,28},{16,0},{20,4},{24,8},{28,12},{1,17},{... | collective-permute-start | bytes 786440 | tf_op jit(solution)/shard_map/ppermute | solution.py:17
  75.7 4.4 %copy-start.5 = (f32[32,101,128]{2,1,0:T(8,128)S(1)}, f32[32,101,128]{2,1,0:T(8,128)}, u32[]{:S(2)}) copy-start(f32[32,101,128]{2,1,0:T(8,128)} %get-tuple-element.422) | copy-start | bytes 4964356 | tf_op jit(solution)/shard_map/while
  86.0 4.4 %copy-start.5 = (f32[32,101,128]{2,1,0:T(8,128)S(1)}, f32[32,101,128]{2,1,0:T(8,128)}, u32[]{:S(2)}) copy-start(f32[32,101,128]{2,1,0:T(8,128)} %get-tuple-element.422) | copy-start | bytes 4964356 | tf_op jit(solution)/shard_map/while
  96.3 4.4 %copy-start.5 = (f32[32,101,128]{2,1,0:T(8,128)S(1)}, f32[32,101,128]{2,1,0:T(8,128)}, u32[]{:S(2)}) copy-start(f32[32,101,128]{2,1,0:T(8,128)} %get-tuple-element.422) | copy-start | bytes 4964356 | tf_op jit(solution)/shard_map/while
  116.8 4.4 %copy-start.5 = (f32[32,101,128]{2,1,0:T(8,128)S(1)}, f32[32,101,128]{2,1,0:T(8,128)}, u32[]{:S(2)}) copy-start(f32[32,101,128]{2,1,0:T(8,128)} %get-tuple-element.422) | copy-start | bytes 4964356 | tf_op jit(solution)/shard_map/while
  127.1 4.4 %copy-start.5 = (f32[32,101,128]{2,1,0:T(8,128)S(1)}, f32[32,101,128]{2,1,0:T(8,128)}, u32[]{:S(2)}) copy-start(f32[32,101,128]{2,1,0:T(8,128)} %get-tuple-element.422) | copy-start | bytes 4964356 | tf_op jit(solution)/shard_map/while
  137.4 4.4 %copy-start.5 = (f32[32,101,128]{2,1,0:T(8,128)S(1)}, f32[32,101,128]{2,1,0:T(8,128)}, u32[]{:S(2)}) copy-start(f32[32,101,128]{2,1,0:T(8,128)} %get-tuple-element.422) | copy-start | bytes 4964356 | tf_op jit(solution)/shard_map/while
  147.7 4.4 %copy-start.5 = (f32[32,101,128]{2,1,0:T(8,128)S(1)}, f32[32,101,128]{2,1,0:T(8,128)}, u32[]{:S(2)}) copy-start(f32[32,101,128]{2,1,0:T(8,128)} %get-tuple-element.422) | copy-start | bytes 4964356 | tf_op jit(solution)/shard_map/while
  158.0 4.4 %copy-start.2 = (f32[32,101,128]{2,1,0:T(8,128)S(1)}, f32[32,101,128]{2,1,0:T(8,128)}, u32[]{:S(2)}) copy-start(f32[32,101,128]{2,1,0:T(8,128)} %get-tuple-element.452) | copy-start | bytes 4964356 | tf_op jit(solution)/shard_map/while
  188.8 4.4 %copy-start.2 = (f32[32,101,128]{2,1,0:T(8,128)S(1)}, f32[32,101,128]{2,1,0:T(8,128)}, u32[]{:S(2)}) copy-start(f32[32,101,128]{2,1,0:T(8,128)} %get-tuple-element.452) | copy-start | bytes 4964356 | tf_op jit(solution)/shard_map/while
  199.1 4.4 %copy-start.2 = (f32[32,101,128]{2,1,0:T(8,128)S(1)}, f32[32,101,128]{2,1,0:T(8,128)}, u32[]{:S(2)}) copy-start(f32[32,101,128]{2,1,0:T(8,128)} %get-tuple-element.452) | copy-start | bytes 4964356 | tf_op jit(solution)/shard_map/while
  240.3 4.4 %copy-start = (f32[32,101,128]{2,1,0:T(8,128)S(1)}, f32[32,101,128]{2,1,0:T(8,128)}, u32[]{:S(2)}) copy-start(f32[32,101,128]{2,1,0:T(8,128)} %get-tuple-element.482) | copy-start | bytes 4964356 | tf_op jit(solution)/shard_map/while
  260.9 4.4 %copy-start = (f32[32,101,128]{2,1,0:T(8,128)S(1)}, f32[32,101,128]{2,1,0:T(8,128)}, u32[]{:S(2)}) copy-start(f32[32,101,128]{2,1,0:T(8,128)} %get-tuple-element.482) | copy-start | bytes 4964356 | tf_op jit(solution)/shard_map/while
  281.6 4.4 %copy-start = (f32[32,101,128]{2,1,0:T(8,128)S(1)}, f32[32,101,128]{2,1,0:T(8,128)}, u32[]{:S(2)}) copy-start(f32[32,101,128]{2,1,0:T(8,128)} %get-tuple-element.482) | copy-start | bytes 4964356 | tf_op jit(solution)/shard_map/while
  (37 other events, 81.7 us)
where the time goes:
time: 328 us; the launch traced here: 326 us
  local copies, waits for them, and re-layouts  217 us (66%)
  matrix products  41.5 us (13%)
  blocking collectives  24.4 us (7%)
  waiting for transfers between devices  16.2 us (5%)
  starting transfers between devices  14.6 us (4%)
  between operations  8.17 us (2%)
    reshape x24, local copies, waits for them, and re-layouts, tile_step(): jnp.tile(extended, (1, lag_count))[:, :lag_count * span_len]  106 us
    another operation x48, local copies, waits for them, and re-layouts, tile_step(): jnp.tile(extended, (1, lag_count))[:, :lag_count * span_len]  42 us
    dot_general x24, matrix products, tile_step(): jnp.einsum('ilw,jw->ilj', toeplitz, window, preferred_element_type=jnp.fl...  40.4 us
    slice x24, local copies, waits for them, and re-layouts, tile_step(): jnp.tile(extended, (1, lag_count))[:, :lag_count * span_len]  29.1 us
    while x96, local copies, waits for them, and re-layouts  28.8 us
    ppermute x7, waiting for transfers between devices, partner_2(): return lax.ppermute(value, axis, pairs)  15.4 us
    all_gather x1, blocking collectives, local(): whole_block = lax.all_gather(my_rows, 'tm', axis=0, tiled=True)  13.8 us
    all_to_all x1, blocking collectives, local(): lax.all_to_all(normalized, 'tm', split_axis=0, concat_axis=1, tiled=True)  10.6 us
  transfers between devices with their start and end apart: 9, of which 6 were waited for; matrix products, arithmetic and copies ran while one was open for 2% of the time, Pallas kernels for 0%

commit v1 on v0

v1 whole, which is shorter than its diff:
```python
import functools

import jax
import jax.numpy as jnp
from jax import lax
from jax.experimental import pallas as pl
from jax.experimental.pallas import tpu as pltpu
from jax.sharding import PartitionSpec as P

AVG_HALF = 64
LAGS = 101
ROUNDS = 3
TILE = 256
EDGE = 128
LAG_GROUP = 26
MESH = pl.DeviceIdType.MESH


def flipped(index, mask):
    bit = 1
    while bit <= mask:
        if mask & bit:
            index = index + bit - 2 * bit * (lax.div(index, bit) % 2)
        bit *= 2
    return index


def gather_kernel(n_sta, n_tm, valid_ref, rec_ref, all_ref, masked, keep_sem, z_send, z_recv, send, recv):
    sta = lax.axis_index("sta")
    tm = lax.axis_index("tm")
    bits = n_sta.bit_length() - 1
    offsets = sorted(range(1, n_tm), key=lambda k: (min(k, n_tm - k), k))

    def tm_at(k):
        return lax.rem(tm + k, n_tm)

    barrier = pltpu.get_barrier_semaphore()
    for b in range(bits):
        pl.semaphore_signal(barrier, inc=1, device_id=(flipped(sta, 1 << b), tm), device_id_type=MESH)
    for k in offsets:
        pl.semaphore_signal(barrier, inc=1, device_id=(sta, tm_at(k)), device_id_type=MESH)

    rows = rec_ref.shape[0]
    row = lax.broadcasted_iota(jnp.int32, (rows, rows), 0)
    col = lax.broadcasted_iota(jnp.int32, (rows, rows), 1)
    keep = jnp.where(row == col, valid_ref[...], 0).astype(jnp.float32).astype(jnp.bfloat16)
    masked[...] = jnp.dot(keep, rec_ref[...], preferred_element_type=jnp.float32).astype(jnp.bfloat16)
    own_copy = pltpu.make_async_copy(masked, all_ref.at[sta, tm], keep_sem)
    own_copy.start()

    pl.semaphore_wait(barrier, bits + n_tm - 1)
    started = []

    def pass_on(mask, k, b):
        there = (flipped(sta, mask), tm_at(k))
        source = masked if (mask, k) == (0, 0) else all_ref.at[there]
        copy = pltpu.make_async_remote_copy(
            src_ref=source,
            dst_ref=all_ref.at[there],
            send_sem=send.at[mask ^ (1 << b), k],
            recv_sem=recv.at[mask ^ (1 << b), k],
            device_id=(flipped(sta, 1 << b), tm),
            device_id_type=MESH,
        )
        copy.start()
        started.append(copy)

    for k in offsets:
        copy = pltpu.make_async_remote_copy(
            src_ref=masked,
            dst_ref=all_ref.at[sta, tm],
            send_sem=z_send.at[k],
            recv_sem=z_recv.at[n_tm - k],
            device_id=(sta, tm_at(k)),
            device_id_type=MESH,
        )
        copy.start()
        started.append(copy)

    def arrival(ref_sem, mask, k):
        there = all_ref.at[flipped(sta, mask), tm_at(k)]
        pltpu.make_async_copy(there, there, ref_sem).wait()

    def dims(position):
        outer = list(range(1, bits))
        turn = position % len(outer) if outer else 0
        return outer[turn:] + outer[:turn]

    def own_ready(position, k):
        if k:
            arrival(z_recv.at[k], 0, k)
        for b in dims(position):
            pass_on(0, k, b)
        if bits:
            pass_on(0, k, 0)

    def forward(position, k, level):
        order = dims(position)
        for sub in range(1 << level):
            mask = 1 << order[level]
            for a in range(level):
                if sub >> a & 1:
                    mask |= 1 << order[a]
            arrival(recv.at[mask, k], mask, k)
            for b in order[level + 1:]:
                pass_on(mask, k, b)
            pass_on(mask, k, 0)

    chunks = [0] + offsets
    levels = max(bits - 1, 0)
    for turn in range(len(chunks) + levels):
        for level in range(levels, -1, -1):
            position = turn - level
            if 0 <= position < len(chunks):
                if level == 0:
                    own_ready(position, chunks[position])
                else:
                    forward(position, chunks[position], level - 1)
    for position, k in enumerate(chunks):
        for mask in range(1, n_sta, 2):
            arrival(recv.at[mask, k], mask, k)
    for copy in started:
        copy.wait_send()
    own_copy.wait()


def gather(records, valid, n_sta, n_tm):
    rows, cols = records.shape
    return pl.pallas_call(
        functools.partial(gather_kernel, n_sta, n_tm),
        out_shape=jax.ShapeDtypeStruct((n_sta, n_tm, rows, cols), records.dtype),
        in_specs=[pl.BlockSpec(memory_space=pltpu.VMEM)] * 2,
        out_specs=pl.BlockSpec(memory_space=pl.ANY),
        scratch_shapes=[
            pltpu.VMEM((rows, cols), records.dtype),
            pltpu.SemaphoreType.DMA,
            pltpu.SemaphoreType.DMA((n_tm,)),
            pltpu.SemaphoreType.DMA((n_tm,)),
            pltpu.SemaphoreType.DMA((n_sta, n_tm)),
            pltpu.SemaphoreType.DMA((n_sta, n_tm)),
        ],
        compiler_params=pltpu.CompilerParams(collective_id=0, has_side_effects=True),
        name="gather_records",
    )(valid, records)


def times_rows(left, right):
    return lax.dot_general(left, right, (((1,), (1,)), ((), ())), preferred_element_type=jnp.float32)


def correlate_kernel(n_tm, where_ref, taps_ref, all_ref, out_ref, raw, tapline, filt, high, low, partners, own, toep, stage, in_sem, out_sem):
    block_rows, cols = all_ref.shape[2], all_ref.shape[3]
    length = n_tm * cols
    own_rows = own.shape[0]
    n_taps = taps_ref.shape[1]
    paired = ROUNDS * block_rows
    copies = []
    for r in range(ROUNDS):
        for c in range(n_tm):
            copies.append(pltpu.make_async_copy(
                all_ref.at[where_ref[r], c],
                raw.at[pl.ds(r * block_rows, block_rows), pl.ds(EDGE + c * cols, cols)],
                in_sem.at[r, c],
            ))
    first = pl.multiple_of(where_ref[ROUNDS + 1] * own_rows, own_rows)
    for c in range(n_tm):
        copies.append(pltpu.make_async_copy(
            all_ref.at[where_ref[ROUNDS], c, pl.ds(first, own_rows), :],
            raw.at[pl.ds(paired, own_rows), pl.ds(EDGE + c * cols, cols)],
            in_sem.at[ROUNDS, c],
        ))
    for copy in copies:
        copy.start()

    for ref in (raw, high, low, own):
        blank = jnp.zeros((ref.shape[0], EDGE), ref.dtype)
        ref[:, :EDGE] = blank
        ref[:, EDGE + length:] = blank
    span = TILE + 2 * EDGE
    tapline[...] = jnp.zeros(tapline.shape, tapline.dtype)
    tapline[0:1, :n_taps] = taps_ref[...]
    line = jnp.broadcast_to(tapline[0:1, :], (TILE, span))
    band = pltpu.roll(line, EDGE - (n_taps - 1) // 2, 1, stride=1, stride_axis=0)
    band_high = band.astype(jnp.bfloat16)
    band_low = (band - band_high.astype(jnp.float32)).astype(jnp.bfloat16)
    ahead = lax.broadcasted_iota(jnp.int32, (TILE, span), 1) - lax.broadcasted_iota(jnp.int32, (TILE, span), 0) - EDGE
    box = jnp.where((ahead >= -AVG_HALF) & (ahead <= AVG_HALF), 1.0, 0.0).astype(jnp.bfloat16)

    for copy in copies:
        copy.wait()
    for t in range(0, length, TILE):
        window = raw[:, t:t + span]
        value = times_rows(window, band_high) + times_rows(window, band_low)
        filt[:, t:t + TILE] = value
        size = jnp.abs(value)
        top = size.astype(jnp.bfloat16)
        high[:, EDGE + t:EDGE + t + TILE] = top
        low[:, EDGE + t:EDGE + t + TILE] = (size - top.astype(jnp.float32)).astype(jnp.bfloat16)
    for t in range(0, length, TILE):
        total = times_rows(high[:, t:t + span], box) + times_rows(low[:, t:t + span], box)
        magnitude = total * (1.0 / (2 * AVG_HALF + 1)) + 1e-5
        normal = (filt[:, t:t + TILE] / magnitude).astype(jnp.bfloat16)
        partners[:, t:t + TILE] = normal[:paired]
        own[:, EDGE + t:EDGE + t + TILE] = normal[paired:]

    factor = float(length) ** -0.5
    half_lags = (LAGS - 1) // 2
    own_wide = own[...]
    results = []
    for g, l0 in enumerate(range(0, LAGS, LAG_GROUP)):
        count = min(LAG_GROUP, LAGS - l0)
        for l in range(count):
            begin = EDGE + half_lags - l0 - l
            toep[(l0 + l) * own_rows:(l0 + l + 1) * own_rows, :] = own_wide[:, begin:begin + length]
        rows = toep[l0 * own_rows:(l0 + count) * own_rows, :]
        sums = (times_rows(rows, partners[...]) * factor).astype(jnp.bfloat16)
        for r in range(ROUNDS):
            part = sums[:, r * block_rows:(r + 1) * block_rows]
            stage[r, l0:l0 + count] = part.reshape(count, own_rows, block_rows)
        result = pltpu.make_async_copy(
            stage.at[:, pl.ds(l0, count)], out_ref.at[:, pl.ds(l0, count)], out_sem.at[g]
        )
        result.start()
        results.append(result)
    for result in results:
        result.wait()


def correlate(everything, where, taps):
    n_sta, n_tm, block_rows, cols = everything.shape
    length = n_tm * cols
    own_rows = block_rows // n_tm
    rows = ROUNDS * block_rows + own_rows
    wide = length + 2 * EDGE
    groups = -(-LAGS // LAG_GROUP)
    bf16 = jnp.bfloat16
    return pl.pallas_call(
        functools.partial(correlate_kernel, n_tm),
        out_shape=jax.ShapeDtypeStruct((ROUNDS, LAGS, own_rows, block_rows), bf16),
        in_specs=[
            pl.BlockSpec(memory_space=pltpu.SMEM),
            pl.BlockSpec(memory_space=pltpu.VMEM),
            pl.BlockSpec(memory_space=pl.ANY),
        ],
        out_specs=pl.BlockSpec(memory_space=pl.ANY),
        scratch_shapes=[
            pltpu.VMEM((rows, wide), bf16),
            pltpu.VMEM((8, TILE + 2 * EDGE), jnp.float32),
            pltpu.VMEM((rows, length), jnp.float32),
            pltpu.VMEM((rows, wide), bf16),
            pltpu.VMEM((rows, wide), bf16),
            pltpu.VMEM((ROUNDS * block_rows, length), bf16),
            pltpu.VMEM((own_rows, wide), bf16),
            pltpu.VMEM((LAGS * own_rows, length), bf16),
            pltpu.VMEM((ROUNDS, LAGS, own_rows, block_rows), bf16),
            pltpu.SemaphoreType.DMA((ROUNDS + 1, n_tm)),
            pltpu.SemaphoreType.DMA((groups,)),
        ],
        compiler_params=pltpu.CompilerParams(vmem_limit_bytes=48 * 2**20),
        name="correlate_blocks",
    )(where, taps, everything)


def local(records, filter_taps, plan, station_valid):
    n_sta, n_tm = lax.axis_size("sta"), lax.axis_size("tm")
    everything = gather(records, station_valid[None, :], n_sta, n_tm)
    sta = lax.axis_index("sta").astype(jnp.int32)
    here = jnp.stack([sta, lax.axis_index("tm").astype(jnp.int32)])
    where = jnp.concatenate([jnp.bitwise_xor(plan, sta), here])
    lagged = correlate(everything, where, filter_taps[None, :])
    return jnp.transpose(lagged, (0, 2, 1, 3))


def solution(mesh):
    return jax.shard_map(
        local,
        mesh=mesh,
        in_specs=(P("sta", "tm"), P(), P(), P("sta")),
        out_specs=P(None, ("sta", "tm"), None, None),
        check_vma=False,
    )
```

time: 328 us -> 39.2 us (0.12)
  local copies, waits for them, and re-layouts: 217 us -> 2.24 us
  matrix products: 41.5 us -> 0 us
  Pallas kernels: 0 us -> 36 us
  blocking collectives: 24.4 us -> 0 us
  waiting for transfers between devices: 16.2 us -> 0 us
  starting transfers between devices: 14.6 us -> 0 us
  between operations: 8.17 us -> 0.02 us
    reshape x26 -> x0, local copies, waits for them, and re-layouts: 106 us -> none  [the longest x24 106 us: tile_step(): jnp.tile(extended, (1, lag_count))[:, :lag_count * span_len]]
    another operation x53 -> x0, local copies, waits for them, and re-layouts: 46.2 us -> none  [the longest x48 42 us: tile_step(): jnp.tile(extended, (1, lag_count))[:, :lag_count * span_len]]
    dot_general x26 -> x0, matrix products: 41.5 us -> none  [the longest x24 40.4 us: tile_step(): jnp.einsum('ilw,jw->ilj', toeplitz, window, preferred_element_type=jnp.fl...]
    pallas_call x0 -> x2, Pallas kernels: none -> 36 us  [the longest x1 28.7 us: gather(): pl.pallas_call(functools.partial(gather_kernel, n_sta, n_tm), out_shape=j...]
    while x97 -> x0, local copies, waits for them, and re-layouts: 30.7 us -> none
    slice x27 -> x0, local copies, waits for them, and re-layouts: 30.6 us -> none  [the longest x24 29.1 us: tile_step(): jnp.tile(extended, (1, lag_count))[:, :lag_count * span_len]]
    ppermute x9 -> x0, waiting for transfers between devices: 16.2 us -> none  [the longest x7 15.4 us: partner_2(): return lax.ppermute(value, axis, pairs)]
    ppermute x9 -> x0, starting transfers between devices: 14.6 us -> none  [the longest x7 8.4 us: partner_2(): return lax.ppermute(value, axis, pairs)]
  transfers between devices with their start and end apart: 9 -> 0, of which waited for: 6 -> 0; matrix products, arithmetic and copies ran while one was open for 2% -> 0% of each run, Pallas kernels for 0% -> 0%
where the time goes in v1:
time: 39.2 us; the launch traced here: 39 us
  Pallas kernels  36 us (92%)
  local copies, waits for them, and re-layouts  2.24 us (6%)
  other arithmetic  0.74 us (2%)
    pallas_call x1, Pallas kernels, gather(): pl.pallas_call(functools.partial(gather_kernel, n_sta, n_tm), out_shape=j...  28.7 us
    pallas_call x1, Pallas kernels, correlate(): pl.pallas_call(functools.partial(correlate_kernel, n_tm), out_shape=jax.S...  7.29 us
    unnamed x4, local copies, waits for them, and re-layouts  2.24 us

profile of v1, /device:TPU:0, one launch (start us, length us, event | category | flops | bytes accessed | tf_op | source)
XLA Modules:
  0.0 39.0 jit_solution(4363944681854698536)
XLA Ops:
  0.0 0.7 %broadcast_xor_fusion = s32[3]{0:T(128)S(1)} fusion(s32[3]{0:T(128)} %param.6, s32[]{:T(128)} %axis_index.23), kind=kLoop, calls=%fused_computation.1 | loop fusion | flops 3 | bytes 28 | tf_op jit(solution)/shard_map/xor | solution.py:269
  0.7 0.1 pad_add_fusion.where_ref
  0.7 28.7 %gather_records.1.all_ref = bf16[8,4,128,256]{3,2,1,0:T(8,128)(2,1)} custom-call(s32[1,128]{1,0:T(1,128)} %bitcast.6, bf16[128,256]{1,0:T(8,128)(2,1)} %rec_ref.1), custom_call_target="tpu_custom_call" | custom-call | tf_op jit(solution)/shard_map/gather_records/pallas_call | solution.py:129
  29.4 0.0 copy-start
  29.4 1.6 %copy-done = bf16[8,4,128,256]{3,2,1,0:T(8,128)(2,1)S(1)} copy-done((bf16[8,4,128,256]{3,2,1,0:T(8,128)(2,1)S(1)}, bf16[8,4,128,256]{3,2,1,0:T(8,128)(2,1)}, u32[]{:S(2)}) %copy-start) | copy-done | bytes 2097176
  31.0 0.0 copy-start.1
  31.0 0.7 %copy-done.1 = f32[127]{0:T(128)S(1)} copy-done((f32[127]{0:T(128)S(1)}, f32[127]{0:T(128)}, u32[]{:S(2)}) %copy-start.1) | copy-done | bytes 532
  31.7 7.3 %correlate_blocks.1 = bf16[3,101,32,128]{3,2,1,0:T(8,128)(2,1)} custom-call(s32[5]{0:T(128)S(1)} %pad_add_fusion.where_ref, f32[1,127]{1,0:T(1,128)S(1)} %bitcast.5, bf16[8,4,128,256]{3,2,1,0:T(8,128)(2,1)S(1)} %copy-done), custom_call_target="tpu_custom_call" | custom-call | tf_op jit(solution)/shard_map/correlate_blocks/pallas_call | solution.py:237
Async XLA Ops:
  29.4 1.6 %copy-start = (bf16[8,4,128,256]{3,2,1,0:T(8,128)(2,1)S(1)}, bf16[8,4,128,256]{3,2,1,0:T(8,128)(2,1)}, u32[]{:S(2)}) copy-start(bf16[8,4,128,256]{3,2,1,0:T(8,128)(2,1)} %gather_records.1.all_ref) | copy-start | bytes 6291460
  31.0 0.7 %copy-start.1 = (f32[127]{0:T(128)S(1)}, f32[127]{0:T(128)}, u32[]{:S(2)}) copy-start(f32[127]{0:T(128)} %param.5) | copy-start | bytes 1528

commit v2 on v1

--- a/solution.py
+++ b/solution.py
@@ -29,16 +29,23 @@
     sta = lax.axis_index("sta")
     tm = lax.axis_index("tm")
     bits = n_sta.bit_length() - 1
-    offsets = sorted(range(1, n_tm), key=lambda k: (min(k, n_tm - k), k))
-
-    def tm_at(k):
-        return lax.rem(tm + k, n_tm)
+    outer = list(range(1, bits))
+
+    def chunk_at(position):
+        chunk = tm
+        for here in range(n_tm):
+            near = sorted(range(n_tm), key=lambda there: (abs(there - here), there))
+            chunk = jnp.where(tm == here, near[position], chunk)
+        return chunk
+
+    chunks = [tm] + [chunk_at(position) for position in range(1, n_tm)]
 
     barrier = pltpu.get_barrier_semaphore()
-    for b in range(bits):
-        pl.semaphore_signal(barrier, inc=1, device_id=(flipped(sta, 1 << b), tm), device_id_type=MESH)
-    for k in offsets:
-        pl.semaphore_signal(barrier, inc=1, device_id=(sta, tm_at(k)), device_id_type=MESH)
+    masks = [1] + list(range(2, n_sta, 2))
+    for mask in masks:
+        pl.semaphore_signal(barrier, inc=1, device_id=(flipped(sta, mask), tm), device_id_type=MESH)
+    for chunk in chunks[1:]:
+        pl.semaphore_signal(barrier, inc=1, device_id=(sta, chunk), device_id_type=MESH)
 
     rows = rec_ref.shape[0]
     row = lax.broadcasted_iota(jnp.int32, (rows, rows), 0)
@@ -48,77 +55,76 @@
     own_copy = pltpu.make_async_copy(masked, all_ref.at[sta, tm], keep_sem)
     own_copy.start()
 
-    pl.semaphore_wait(barrier, bits + n_tm - 1)
+    pl.semaphore_wait(barrier, len(masks) + n_tm - 1)
     started = []
 
-    def pass_on(mask, k, b):
-        there = (flipped(sta, mask), tm_at(k))
-        source = masked if (mask, k) == (0, 0) else all_ref.at[there]
+    def pass_on(mask, position, jump):
+        there = (flipped(sta, mask), chunks[position])
         copy = pltpu.make_async_remote_copy(
-            src_ref=source,
+            src_ref=masked if mask == position == 0 else all_ref.at[there],
             dst_ref=all_ref.at[there],
-            send_sem=send.at[mask ^ (1 << b), k],
-            recv_sem=recv.at[mask ^ (1 << b), k],
-            device_id=(flipped(sta, 1 << b), tm),
+            send_sem=send.at[mask ^ jump, position],
+            recv_sem=recv.at[mask ^ jump, position],
+            device_id=(flipped(sta, jump), tm),
             device_id_type=MESH,
         )
         copy.start()
         started.append(copy)
 
-    for k in offsets:
+    def arrival(sem, mask, position):
+        there = all_ref.at[flipped(sta, mask), chunks[position]]
+        pltpu.make_async_copy(there, there, sem).wait()
+
+    for position in range(1, n_tm):
         copy = pltpu.make_async_remote_copy(
             src_ref=masked,
             dst_ref=all_ref.at[sta, tm],
-            send_sem=z_send.at[k],
-            recv_sem=z_recv.at[n_tm - k],
-            device_id=(sta, tm_at(k)),
+            send_sem=z_send.at[position],
+            recv_sem=z_recv.at[tm],
+            device_id=(sta, chunks[position]),
             device_id_type=MESH,
         )
         copy.start()
         started.append(copy)
 
-    def arrival(ref_sem, mask, k):
-        there = all_ref.at[flipped(sta, mask), tm_at(k)]
-        pltpu.make_async_copy(there, there, ref_sem).wait()
-
-    def dims(position):
-        outer = list(range(1, bits))
-        turn = position % len(outer) if outer else 0
+    def direct(position):
+        return position == n_tm - 1 or len(outer) != 2
+
+    def first_bits(position):
+        turn = position % 2
         return outer[turn:] + outer[:turn]
 
-    def own_ready(position, k):
-        if k:
-            arrival(z_recv.at[k], 0, k)
-        for b in dims(position):
-            pass_on(0, k, b)
-        if bits:
-            pass_on(0, k, 0)
-
-    def forward(position, k, level):
-        order = dims(position)
-        for sub in range(1 << level):
-            mask = 1 << order[level]
-            for a in range(level):
-                if sub >> a & 1:
-                    mask |= 1 << order[a]
-            arrival(recv.at[mask, k], mask, k)
-            for b in order[level + 1:]:
-                pass_on(mask, k, b)
-            pass_on(mask, k, 0)
-
-    chunks = [0] + offsets
-    levels = max(bits - 1, 0)
-    for turn in range(len(chunks) + levels):
-        for level in range(levels, -1, -1):
-            position = turn - level
-            if 0 <= position < len(chunks):
-                if level == 0:
-                    own_ready(position, chunks[position])
-                else:
-                    forward(position, chunks[position], level - 1)
-    for position, k in enumerate(chunks):
+    def own_ready(position):
+        if position:
+            arrival(z_recv.at[chunks[position]], 0, position)
+        if direct(position):
+            for mask in range(2, n_sta, 2):
+                pass_on(0, position, mask)
+        else:
+            for b in first_bits(position):
+                pass_on(0, position, 1 << b)
+        pass_on(0, position, 1)
+
+    def relay(position):
+        if not direct(position):
+            first, second = first_bits(position)
+            arrival(recv.at[1 << first, position], 1 << first, position)
+            pass_on(1 << first, position, 1 << second)
+            pass_on(1 << first, position, 1)
+
+    for position in range(n_tm + 1):
+        if position < n_tm:
+            own_ready(position)
+        if position:
+            relay(position - 1)
+    for position in range(n_tm):
+        for mask in range(2, n_sta, 2):
+            if direct(position) or mask != 1 << first_bits(position)[0]:
+                arrival(recv.at[mask, position], mask, position)
+                pass_on(mask, position, 1)
+    for position in range(n_tm):
         for mask in range(1, n_sta, 2):
-            arrival(recv.at[mask, k], mask, k)
+            arrival(recv.at[mask, position], mask, position)
     for copy in started:
         copy.wait_send()
     own_copy.wait()
@@ -139,7 +145,9 @@
             pltpu.SemaphoreType.DMA((n_sta, n_tm)),
             pltpu.SemaphoreType.DMA((n_sta, n_tm)),
         ],
-        compiler_params=pltpu.CompilerParams(collective_id=0, has_side_effects=True),
+        compiler_params=pltpu.CompilerParams(
+            collective_id=0, has_side_effects=True, vmem_limit_bytes=60 * 2**20
+        ),
         name="gather_records",
     )(valid, records)
 
@@ -148,24 +156,25 @@
     return lax.dot_general(left, right, (((1,), (1,)), ((), ())), preferred_element_type=jnp.float32)
 
 
-def correlate_kernel(n_tm, where_ref, taps_ref, all_ref, out_ref, raw, tapline, filt, high, low, partners, own, toep, stage, in_sem, out_sem):
+def correlate_kernel(n_tm, plan_ref, taps_ref, all_ref, out_ref, raw, tapline, filt, high, low, partners, own, toep, stage, in_sem, out_sem):
     block_rows, cols = all_ref.shape[2], all_ref.shape[3]
     length = n_tm * cols
     own_rows = own.shape[0]
     n_taps = taps_ref.shape[1]
     paired = ROUNDS * block_rows
+    sta = lax.axis_index("sta")
     copies = []
     for r in range(ROUNDS):
         for c in range(n_tm):
             copies.append(pltpu.make_async_copy(
-                all_ref.at[where_ref[r], c],
+                all_ref.at[jnp.bitwise_xor(plan_ref[r], sta), c],
                 raw.at[pl.ds(r * block_rows, block_rows), pl.ds(EDGE + c * cols, cols)],
                 in_sem.at[r, c],
             ))
-    first = pl.multiple_of(where_ref[ROUNDS + 1] * own_rows, own_rows)
+    first = pl.multiple_of(lax.axis_index("tm") * own_rows, own_rows)
     for c in range(n_tm):
         copies.append(pltpu.make_async_copy(
-            all_ref.at[where_ref[ROUNDS], c, pl.ds(first, own_rows), :],
+            all_ref.at[sta, c, pl.ds(first, own_rows), :],
             raw.at[pl.ds(paired, own_rows), pl.ds(EDGE + c * cols, cols)],
             in_sem.at[ROUNDS, c],
         ))
@@ -226,7 +235,7 @@
         result.wait()
 
 
-def correlate(everything, where, taps):
+def correlate(everything, plan, taps):
     n_sta, n_tm, block_rows, cols = everything.shape
     length = n_tm * cols
     own_rows = block_rows // n_tm
@@ -256,18 +265,15 @@
             pltpu.SemaphoreType.DMA((ROUNDS + 1, n_tm)),
             pltpu.SemaphoreType.DMA((groups,)),
         ],
-        compiler_params=pltpu.CompilerParams(vmem_limit_bytes=48 * 2**20),
+        compiler_params=pltpu.CompilerParams(vmem_limit_bytes=60 * 2**20),
         name="correlate_blocks",
-    )(where, taps, everything)
+    )(plan, taps, everything)
 
 
 def local(records, filter_taps, plan, station_valid):
     n_sta, n_tm = lax.axis_size("sta"), lax.axis_size("tm")
     everything = gather(records, station_valid[None, :], n_sta, n_tm)
-    sta = lax.axis_index("sta").astype(jnp.int32)
-    here = jnp.stack([sta, lax.axis_index("tm").astype(jnp.int32)])
-    where = jnp.concatenate([jnp.bitwise_xor(plan, sta), here])
-    lagged = correlate(everything, where, filter_taps[None, :])
+    lagged = correlate(everything, plan, filter_taps[None, :])
     return jnp.transpose(lagged, (0, 2, 1, 3))
 
 

time: 39.2 us -> 31.5 us (0.80)
  Pallas kernels: 36 us -> 31.2 us
  local copies, waits for them, and re-layouts: 2.24 us -> 0 us
  other arithmetic: 0.74 us -> 0 us
    pallas_call x1, Pallas kernels: 28.7 us -> 22.9 us  [gather(): pl.pallas_call(functools.partial(gather_kernel, n_sta, n_tm), out_shape=j...]
    unnamed x4 -> x0, local copies, waits for them, and re-layouts: 2.24 us -> none
    pallas_call x1, Pallas kernels: 7.29 us -> 8.35 us  [correlate(): pl.pallas_call(functools.partial(correlate_kernel, n_tm), out_shape=jax.S...]
    xor x1 -> x0, other arithmetic: 0.66 us -> none  [local(): where = jnp.concatenate([jnp.bitwise_xor(plan, sta), here])]
where the time goes in v2:
time: 31.5 us; the launch traced here: 31.2 us
  Pallas kernels  31.2 us (99%)
    pallas_call x1, Pallas kernels, gather(): pl.pallas_call(functools.partial(gather_kernel, n_sta, n_tm), out_shape=j...  22.9 us
    pallas_call x1, Pallas kernels, correlate(): pl.pallas_call(functools.partial(correlate_kernel, n_tm), out_shape=jax.S...  8.35 us

profile of v2, /device:TPU:0, one launch (start us, length us, event | category | flops | bytes accessed | tf_op | source)
XLA Modules:
  0.0 31.2 jit_solution(5772425170801209020)
XLA Ops:
  0.0 22.9 %gather_records.1.all_ref = bf16[8,4,128,256]{3,2,1,0:T(8,128)(2,1)} custom-call(s32[1,128]{1,0:T(1,128)} %bitcast.3, bf16[128,256]{1,0:T(8,128)(2,1)} %rec_ref.1), custom_call_target="tpu_custom_call" | custom-call | tf_op jit(solution)/shard_map/gather_records/pallas_call | solution.py:135
  22.9 8.3 %correlate_blocks.1 = bf16[3,101,32,128]{3,2,1,0:T(8,128)(2,1)} custom-call(s32[3]{0:T(128)} %plan_ref.1, f32[1,127]{1,0:T(1,128)} %bitcast.4, bf16[8,4,128,256]{3,2,1,0:T(8,128)(2,1)} %gather_records.1.all_ref), custom_call_target="tpu_custom_call" | custom-call | tf_op jit(solution)/shard_map/correlate_blocks/pallas_call | solution.py:246

commit v3 on v2

--- a/solution.py
+++ b/solution.py
@@ -25,7 +25,7 @@
     return index
 
 
-def gather_kernel(n_sta, n_tm, valid_ref, rec_ref, all_ref, masked, keep_sem, z_send, z_recv, send, recv):
+def gather_kernel(n_sta, n_tm, valid_ref, rec_ref, all_ref, valid, rec, held, in_sem, keep, z_send, z_recv, send, recv):
     sta = lax.axis_index("sta")
     tm = lax.axis_index("tm")
     bits = n_sta.bit_length() - 1
@@ -39,30 +39,45 @@
         return chunk
 
     chunks = [tm] + [chunk_at(position) for position in range(1, n_tm)]
+    inputs = [
+        pltpu.make_async_copy(valid_ref, valid, in_sem.at[0]),
+        pltpu.make_async_copy(rec_ref, rec, in_sem.at[1]),
+    ]
+    for copy in inputs:
+        copy.start()
 
     barrier = pltpu.get_barrier_semaphore()
     masks = [1] + list(range(2, n_sta, 2))
+    for chunk in chunks[1:]:
+        pl.semaphore_signal(barrier, inc=1, device_id=(sta, chunk), device_id_type=MESH)
     for mask in masks:
         pl.semaphore_signal(barrier, inc=1, device_id=(flipped(sta, mask), tm), device_id_type=MESH)
-    for chunk in chunks[1:]:
-        pl.semaphore_signal(barrier, inc=1, device_id=(sta, chunk), device_id_type=MESH)
-
-    rows = rec_ref.shape[0]
+
+    for copy in inputs:
+        copy.wait()
+    rows = rec.shape[0]
     row = lax.broadcasted_iota(jnp.int32, (rows, rows), 0)
     col = lax.broadcasted_iota(jnp.int32, (rows, rows), 1)
-    keep = jnp.where(row == col, valid_ref[...], 0).astype(jnp.float32).astype(jnp.bfloat16)
-    masked[...] = jnp.dot(keep, rec_ref[...], preferred_element_type=jnp.float32).astype(jnp.bfloat16)
-    own_copy = pltpu.make_async_copy(masked, all_ref.at[sta, tm], keep_sem)
-    own_copy.start()
+    alive = jnp.where(row == col, valid[...], 0).astype(jnp.float32).astype(jnp.bfloat16)
+    held[0, tm] = jnp.dot(alive, rec[...], preferred_element_type=jnp.float32).astype(jnp.bfloat16)
 
     pl.semaphore_wait(barrier, len(masks) + n_tm - 1)
     started = []
+    kept = []
+
+    def slot(mask, position):
+        if mask & 1:
+            return all_ref.at[flipped(sta, mask), chunks[position]]
+        return held.at[mask // 2, chunks[position]]
 
     def pass_on(mask, position, jump):
-        there = (flipped(sta, mask), chunks[position])
+        if jump & 1:
+            target = all_ref.at[flipped(sta, mask), chunks[position]]
+        else:
+            target = held.at[(mask ^ jump) // 2, chunks[position]]
         copy = pltpu.make_async_remote_copy(
-            src_ref=masked if mask == position == 0 else all_ref.at[there],
-            dst_ref=all_ref.at[there],
+            src_ref=slot(mask, position),
+            dst_ref=target,
             send_sem=send.at[mask ^ jump, position],
             recv_sem=recv.at[mask ^ jump, position],
             device_id=(flipped(sta, jump), tm),
@@ -72,13 +87,23 @@
         started.append(copy)
 
     def arrival(sem, mask, position):
-        there = all_ref.at[flipped(sta, mask), chunks[position]]
+        there = slot(mask, position)
         pltpu.make_async_copy(there, there, sem).wait()
+
+    def to_core(mask, position):
+        pass_on(mask, position, 1)
+        copy = pltpu.make_async_copy(
+            held.at[mask // 2, chunks[position]],
+            all_ref.at[flipped(sta, mask), chunks[position]],
+            keep.at[mask // 2, position],
+        )
+        copy.start()
+        kept.append(copy)
 
     for position in range(1, n_tm):
         copy = pltpu.make_async_remote_copy(
-            src_ref=masked,
-            dst_ref=all_ref.at[sta, tm],
+            src_ref=held.at[0, tm],
+            dst_ref=held.at[0, tm],
             send_sem=z_send.at[position],
             recv_sem=z_recv.at[tm],
             device_id=(sta, chunks[position]),
@@ -103,43 +128,53 @@
         else:
             for b in first_bits(position):
                 pass_on(0, position, 1 << b)
-        pass_on(0, position, 1)
-
-    def relay(position):
+        to_core(0, position)
+
+    def neighbours(position):
         if not direct(position):
             first, second = first_bits(position)
             arrival(recv.at[1 << first, position], 1 << first, position)
             pass_on(1 << first, position, 1 << second)
-            pass_on(1 << first, position, 1)
-
-    for position in range(n_tm + 1):
-        if position < n_tm:
-            own_ready(position)
-        if position:
-            relay(position - 1)
-    for position in range(n_tm):
+            to_core(1 << first, position)
+            arrival(recv.at[1 << second, position], 1 << second, position)
+            to_core(1 << second, position)
+
+    def far(position):
         for mask in range(2, n_sta, 2):
-            if direct(position) or mask != 1 << first_bits(position)[0]:
+            if direct(position) or mask == sum(1 << b for b in outer):
                 arrival(recv.at[mask, position], mask, position)
-                pass_on(mask, position, 1)
+                to_core(mask, position)
+
+    for turn in range(n_tm + 2):
+        if turn < n_tm:
+            own_ready(turn)
+        if 1 <= turn <= n_tm:
+            neighbours(turn - 1)
+        if turn >= 2:
+            far(turn - 2)
     for position in range(n_tm):
         for mask in range(1, n_sta, 2):
             arrival(recv.at[mask, position], mask, position)
     for copy in started:
         copy.wait_send()
-    own_copy.wait()
+    for copy in kept:
+        copy.wait()
 
 
 def gather(records, valid, n_sta, n_tm):
     rows, cols = records.shape
+    half = max(n_sta // 2, 1)
     return pl.pallas_call(
         functools.partial(gather_kernel, n_sta, n_tm),
         out_shape=jax.ShapeDtypeStruct((n_sta, n_tm, rows, cols), records.dtype),
-        in_specs=[pl.BlockSpec(memory_space=pltpu.VMEM)] * 2,
+        in_specs=[pl.BlockSpec(memory_space=pl.ANY)] * 2,
         out_specs=pl.BlockSpec(memory_space=pl.ANY),
         scratch_shapes=[
+            pltpu.VMEM(valid.shape, valid.dtype),
             pltpu.VMEM((rows, cols), records.dtype),
-            pltpu.SemaphoreType.DMA,
+            pltpu.VMEM((half, n_tm, rows, cols), records.dtype),
+            pltpu.SemaphoreType.DMA((2,)),
+            pltpu.SemaphoreType.DMA((half, n_tm)),
             pltpu.SemaphoreType.DMA((n_tm,)),
             pltpu.SemaphoreType.DMA((n_tm,)),
             pltpu.SemaphoreType.DMA((n_sta, n_tm)),

time: 31.5 us -> 29.8 us (0.946)
  Pallas kernels: 31.2 us -> 29.6 us
    pallas_call x1, Pallas kernels: 22.9 us -> 21.3 us  [gather(): pl.pallas_call(functools.partial(gather_kernel, n_sta, n_tm), out_shape=j...]
where the time goes in v3:
time: 29.8 us; the launch traced here: 29.6 us
  Pallas kernels  29.6 us (99%)
    pallas_call x1, Pallas kernels, gather(): pl.pallas_call(functools.partial(gather_kernel, n_sta, n_tm), out_shape=j...  21.3 us
    pallas_call x1, Pallas kernels, correlate(): pl.pallas_call(functools.partial(correlate_kernel, n_tm), out_shape=jax.S...  8.35 us

profile of v3, /device:TPU:0, one launch (start us, length us, event | category | flops | bytes accessed | tf_op | source)
XLA Modules:
  0.0 29.6 jit_solution(4398112639400055873)
XLA Ops:
  0.0 21.3 %gather_records.1.all_ref = bf16[8,4,128,256]{3,2,1,0:T(8,128)(2,1)} custom-call(s32[1,128]{1,0:T(1,128)} %bitcast.3, bf16[128,256]{1,0:T(8,128)(2,1)} %rec_ref.1), custom_call_target="tpu_custom_call" | custom-call | tf_op jit(solution)/shard_map/gather_records/pallas_call | solution.py:167
  21.3 8.3 %correlate_blocks.1 = bf16[3,101,32,128]{3,2,1,0:T(8,128)(2,1)} custom-call(s32[3]{0:T(128)} %plan_ref.1, f32[1,127]{1,0:T(1,128)} %bitcast.4, bf16[8,4,128,256]{3,2,1,0:T(8,128)(2,1)} %gather_records.1.all_ref), custom_call_target="tpu_custom_call" | custom-call | tf_op jit(solution)/shard_map/correlate_blocks/pallas_call | solution.py:281

commit v4 on v3

--- a/solution.py
+++ b/solution.py
@@ -25,7 +25,53 @@
     return index
 
 
-def gather_kernel(n_sta, n_tm, valid_ref, rec_ref, all_ref, valid, rec, held, in_sem, keep, z_send, z_recv, send, recv):
+def times_rows(left, right):
+    return lax.dot_general(left, right, (((1,), (1,)), ((), ())), preferred_element_type=jnp.float32)
+
+
+def bands(taps_ref, tapline):
+    n_taps = taps_ref.shape[1]
+    span = TILE + 2 * EDGE
+    tapline[...] = jnp.zeros(tapline.shape, tapline.dtype)
+    tapline[0:1, :n_taps] = taps_ref[...]
+    line = jnp.broadcast_to(tapline[0:1, :], (TILE, span))
+    band = pltpu.roll(line, EDGE - (n_taps - 1) // 2, 1, stride=1, stride_axis=0)
+    high = band.astype(jnp.bfloat16)
+    low = (band - high.astype(jnp.float32)).astype(jnp.bfloat16)
+    ahead = lax.broadcasted_iota(jnp.int32, (TILE, span), 1) - lax.broadcasted_iota(jnp.int32, (TILE, span), 0) - EDGE
+    box = jnp.where((ahead >= -AVG_HALF) & (ahead <= AVG_HALF), 1.0, 0.0).astype(jnp.bfloat16)
+    return high, low, box
+
+
+def clear_edges(length, *refs):
+    for ref in refs:
+        blank = jnp.zeros((ref.shape[0], EDGE), ref.dtype)
+        ref[:, :EDGE] = blank
+        ref[:, EDGE + length:] = blank
+
+
+def normalise(length, coeffs, raw, filt, size, out, out_edge):
+    band_high, band_low, box = coeffs
+    span = TILE + 2 * EDGE
+    for t in range(0, length, TILE):
+        window = raw[:, t:t + span]
+        value = times_rows(window, band_high) + times_rows(window, band_low)
+        filt[:, t:t + TILE] = value
+        size[:, EDGE + t:EDGE + t + TILE] = jnp.abs(value).astype(jnp.bfloat16)
+    for t in range(0, length, TILE):
+        magnitude = times_rows(size[:, t:t + span], box) * (1.0 / (2 * AVG_HALF + 1)) + 1e-5
+        out[:, out_edge + t:out_edge + t + TILE] = (filt[:, t:t + TILE] / magnitude).astype(jnp.bfloat16)
+
+
+def lag_groups():
+    return [(l0, min(LAG_GROUP, LAGS - l0)) for l0 in range(0, LAGS, LAG_GROUP)]
+
+
+def gather_kernel(
+    n_sta, n_tm, taps_ref, valid_ref, rec_ref, all_ref, toep_ref,
+    valid, rec, held, tapline, raw, filt, size, own, toep,
+    in_sem, keep, z_send, z_recv, send, recv, toep_sem,
+):
     sta = lax.axis_index("sta")
     tm = lax.axis_index("tm")
     bits = n_sta.bit_length() - 1
@@ -60,6 +106,11 @@
     col = lax.broadcasted_iota(jnp.int32, (rows, rows), 1)
     alive = jnp.where(row == col, valid[...], 0).astype(jnp.float32).astype(jnp.bfloat16)
     held[0, tm] = jnp.dot(alive, rec[...], preferred_element_type=jnp.float32).astype(jnp.bfloat16)
+
+    own_rows, cols = own.shape[0], rec.shape[1]
+    length = n_tm * cols
+    clear_edges(length, raw, size, own)
+    coeffs = bands(taps_ref, tapline)
 
     pl.semaphore_wait(barrier, len(masks) + n_tm - 1)
     started = []
@@ -145,6 +196,24 @@
                 arrival(recv.at[mask, position], mask, position)
                 to_core(mask, position)
 
+    def normalise_own():
+        first = pl.multiple_of(tm * own_rows, own_rows)
+        for c in range(n_tm):
+            raw[:, EDGE + c * cols:EDGE + (c + 1) * cols] = held[0, c, pl.ds(first, own_rows), :]
+        normalise(length, coeffs, raw, filt, size, own, EDGE)
+
+    def lagged_rows(group):
+        l0, count = lag_groups()[group]
+        own_wide = own[...]
+        for l in range(l0, l0 + count):
+            begin = EDGE + (LAGS - 1) // 2 - l
+            toep[l * own_rows:(l + 1) * own_rows, :] = own_wide[:, begin:begin + length]
+        part = pl.ds(l0 * own_rows, count * own_rows)
+        copy = pltpu.make_async_copy(toep.at[part], toep_ref.at[part], toep_sem.at[group])
+        copy.start()
+        kept.append(copy)
+
+    work = [normalise_own] + [functools.partial(lagged_rows, g) for g in range(len(lag_groups()))]
     for turn in range(n_tm + 2):
         if turn < n_tm:
             own_ready(turn)
@@ -152,6 +221,10 @@
             neighbours(turn - 1)
         if turn >= 2:
             far(turn - 2)
+        if turn >= n_tm - 1:
+            work.pop(0)()
+    for step in work:
+        step()
     for position in range(n_tm):
         for mask in range(1, n_sta, 2):
             arrival(recv.at[mask, position], mask, position)
@@ -161,42 +234,49 @@
         copy.wait()
 
 
-def gather(records, valid, n_sta, n_tm):
+def gather(records, valid, taps, n_sta, n_tm):
     rows, cols = records.shape
+    own_rows, length = rows // n_tm, n_tm * cols
+    wide = length + 2 * EDGE
+    bf16 = jnp.bfloat16
     half = max(n_sta // 2, 1)
     return pl.pallas_call(
         functools.partial(gather_kernel, n_sta, n_tm),
-        out_shape=jax.ShapeDtypeStruct((n_sta, n_tm, rows, cols), records.dtype),
-        in_specs=[pl.BlockSpec(memory_space=pl.ANY)] * 2,
-        out_specs=pl.BlockSpec(memory_space=pl.ANY),
+        out_shape=[
+            jax.ShapeDtypeStruct((n_sta, n_tm, rows, cols), records.dtype),
+            jax.ShapeDtypeStruct((LAGS * own_rows, length), bf16),
+        ],
+        in_specs=[pl.BlockSpec(memory_space=pltpu.VMEM)] + [pl.BlockSpec(memory_space=pl.ANY)] * 2,
+        out_specs=[pl.BlockSpec(memory_space=pl.ANY)] * 2,
         scratch_shapes=[
             pltpu.VMEM(valid.shape, valid.dtype),
             pltpu.VMEM((rows, cols), records.dtype),
             pltpu.VMEM((half, n_tm, rows, cols), records.dtype),
+            pltpu.VMEM((8, TILE + 2 * EDGE), jnp.float32),
+            pltpu.VMEM((own_rows, wide), bf16),
+            pltpu.VMEM((own_rows, length), jnp.float32),
+            pltpu.VMEM((own_rows, wide), bf16),
+            pltpu.VMEM((own_rows, wide), bf16),
+            pltpu.VMEM((LAGS * own_rows, length), bf16),
             pltpu.SemaphoreType.DMA((2,)),
             pltpu.SemaphoreType.DMA((half, n_tm)),
             pltpu.SemaphoreType.DMA((n_tm,)),
             pltpu.SemaphoreType.DMA((n_tm,)),
             pltpu.SemaphoreType.DMA((n_sta, n_tm)),
             pltpu.SemaphoreType.DMA((n_sta, n_tm)),
+            pltpu.SemaphoreType.DMA((len(lag_groups()),)),
         ],
         compiler_params=pltpu.CompilerParams(
             collective_id=0, has_side_effects=True, vmem_limit_bytes=60 * 2**20
         ),
         name="gather_records",
-    )(valid, records)
-
-
-def times_rows(left, right):
-    return lax.dot_general(left, right, (((1,), (1,)), ((), ())), preferred_element_type=jnp.float32)
-
-
-def correlate_kernel(n_tm, plan_ref, taps_ref, all_ref, out_ref, raw, tapline, filt, high, low, partners, own, toep, stage, in_sem, out_sem):
+    )(taps, valid, records)
+
+
+def correlate_kernel(n_tm, plan_ref, taps_ref, all_ref, toep_ref, out_ref, raw, tapline, filt, size, partners, toep, stage, in_sem, toep_sem, out_sem):
     block_rows, cols = all_ref.shape[2], all_ref.shape[3]
     length = n_tm * cols
-    own_rows = own.shape[0]
-    n_taps = taps_ref.shape[1]
-    paired = ROUNDS * block_rows
+    own_rows = toep.shape[0] // LAGS
     sta = lax.axis_index("sta")
     copies = []
     for r in range(ROUNDS):
@@ -206,56 +286,23 @@
                 raw.at[pl.ds(r * block_rows, block_rows), pl.ds(EDGE + c * cols, cols)],
                 in_sem.at[r, c],
             ))
-    first = pl.multiple_of(lax.axis_index("tm") * own_rows, own_rows)
-    for c in range(n_tm):
-        copies.append(pltpu.make_async_copy(
-            all_ref.at[sta, c, pl.ds(first, own_rows), :],
-            raw.at[pl.ds(paired, own_rows), pl.ds(EDGE + c * cols, cols)],
-            in_sem.at[ROUNDS, c],
-        ))
-    for copy in copies:
-        copy.start()
-
-    for ref in (raw, high, low, own):
-        blank = jnp.zeros((ref.shape[0], EDGE), ref.dtype)
-        ref[:, :EDGE] = blank
-        ref[:, EDGE + length:] = blank
-    span = TILE + 2 * EDGE
-    tapline[...] = jnp.zeros(tapline.shape, tapline.dtype)
-    tapline[0:1, :n_taps] = taps_ref[...]
-    line = jnp.broadcast_to(tapline[0:1, :], (TILE, span))
-    band = pltpu.roll(line, EDGE - (n_taps - 1) // 2, 1, stride=1, stride_axis=0)
-    band_high = band.astype(jnp.bfloat16)
-    band_low = (band - band_high.astype(jnp.float32)).astype(jnp.bfloat16)
-    ahead = lax.broadcasted_iota(jnp.int32, (TILE, span), 1) - lax.broadcasted_iota(jnp.int32, (TILE, span), 0) - EDGE
-    box = jnp.where((ahead >= -AVG_HALF) & (ahead <= AVG_HALF), 1.0, 0.0).astype(jnp.bfloat16)
-
+    toep_copies = []
+    for g, (l0, count) in enumerate(lag_groups()):
+        part = pl.ds(l0 * own_rows, count * own_rows)
+        toep_copies.append(pltpu.make_async_copy(toep_ref.at[part], toep.at[part], toep_sem.at[g]))
+    for copy in copies + toep_copies:
+        copy.start()
+
+    clear_edges(length, raw, size)
+    coeffs = bands(taps_ref, tapline)
     for copy in copies:
         copy.wait()
-    for t in range(0, length, TILE):
-        window = raw[:, t:t + span]
-        value = times_rows(window, band_high) + times_rows(window, band_low)
-        filt[:, t:t + TILE] = value
-        size = jnp.abs(value)
-        top = size.astype(jnp.bfloat16)
-        high[:, EDGE + t:EDGE + t + TILE] = top
-        low[:, EDGE + t:EDGE + t + TILE] = (size - top.astype(jnp.float32)).astype(jnp.bfloat16)
-    for t in range(0, length, TILE):
-        total = times_rows(high[:, t:t + span], box) + times_rows(low[:, t:t + span], box)
-        magnitude = total * (1.0 / (2 * AVG_HALF + 1)) + 1e-5
-        normal = (filt[:, t:t + TILE] / magnitude).astype(jnp.bfloat16)
-        partners[:, t:t + TILE] = normal[:paired]
-        own[:, EDGE + t:EDGE + t + TILE] = normal[paired:]
+    normalise(length, coeffs, raw, filt, size, partners, 0)
 
     factor = float(length) ** -0.5
-    half_lags = (LAGS - 1) // 2
-    own_wide = own[...]
     results = []
-    for g, l0 in enumerate(range(0, LAGS, LAG_GROUP)):
-        count = min(LAG_GROUP, LAGS - l0)
-        for l in range(count):
-            begin = EDGE + half_lags - l0 - l
-            toep[(l0 + l) * own_rows:(l0 + l + 1) * own_rows, :] = own_wide[:, begin:begin + length]
+    for g, (l0, count) in enumerate(lag_groups()):
+        toep_copies[g].wait()
         rows = toep[l0 * own_rows:(l0 + count) * own_rows, :]
         sums = (times_rows(rows, partners[...]) * factor).astype(jnp.bfloat16)
         for r in range(ROUNDS):
@@ -270,13 +317,12 @@
         result.wait()
 
 
-def correlate(everything, plan, taps):
+def correlate(everything, toep, plan, taps):
     n_sta, n_tm, block_rows, cols = everything.shape
     length = n_tm * cols
     own_rows = block_rows // n_tm
-    rows = ROUNDS * block_rows + own_rows
+    rows = ROUNDS * block_rows
     wide = length + 2 * EDGE
-    groups = -(-LAGS // LAG_GROUP)
     bf16 = jnp.bfloat16
     return pl.pallas_call(
         functools.partial(correlate_kernel, n_tm),
@@ -285,6 +331,7 @@
             pl.BlockSpec(memory_space=pltpu.SMEM),
             pl.BlockSpec(memory_space=pltpu.VMEM),
             pl.BlockSpec(memory_space=pl.ANY),
+            pl.BlockSpec(memory_space=pl.ANY),
         ],
         out_specs=pl.BlockSpec(memory_space=pl.ANY),
         scratch_shapes=[
@@ -292,23 +339,23 @@
             pltpu.VMEM((8, TILE + 2 * EDGE), jnp.float32),
             pltpu.VMEM((rows, length), jnp.float32),
             pltpu.VMEM((rows, wide), bf16),
-            pltpu.VMEM((rows, wide), bf16),
-            pltpu.VMEM((ROUNDS * block_rows, length), bf16),
-            pltpu.VMEM((own_rows, wide), bf16),
-            pltpu.VMEM((LAGS * own_rows, length), bf16),
+            pltpu.VMEM((rows, length), bf16),
+            pltpu.VMEM(toep.shape, bf16),
             pltpu.VMEM((ROUNDS, LAGS, own_rows, block_rows), bf16),
-            pltpu.SemaphoreType.DMA((ROUNDS + 1, n_tm)),
-            pltpu.SemaphoreType.DMA((groups,)),
+            pltpu.SemaphoreType.DMA((ROUNDS, n_tm)),
+            pltpu.SemaphoreType.DMA((len(lag_groups()),)),
+            pltpu.SemaphoreType.DMA((len(lag_groups()),)),
         ],
         compiler_params=pltpu.CompilerParams(vmem_limit_bytes=60 * 2**20),
         name="correlate_blocks",
-    )(plan, taps, everything)
+    )(plan, taps, everything, toep)
 
 
 def local(records, filter_taps, plan, station_valid):
     n_sta, n_tm = lax.axis_size("sta"), lax.axis_size("tm")
-    everything = gather(records, station_valid[None, :], n_sta, n_tm)
-    lagged = correlate(everything, plan, filter_taps[None, :])
+    taps = filter_taps[None, :]
+    everything, toep = gather(records, station_valid[None, :], taps, n_sta, n_tm)
+    lagged = correlate(everything, toep, plan, taps)
     return jnp.transpose(lagged, (0, 2, 1, 3))
 
 

time: 29.8 us -> 33.8 us (1.13)
  Pallas kernels: 29.6 us -> 33.6 us
    pallas_call x1, Pallas kernels: 21.3 us -> 24.1 us  [gather(): pl.pallas_call(functools.partial(gather_kernel, n_sta, n_tm), out_shape=[...]
    pallas_call x1, Pallas kernels: 8.35 us -> 9.54 us  [correlate(): pl.pallas_call(functools.partial(correlate_kernel, n_tm), out_shape=jax.S...]
where the time goes in v4:
time: 33.8 us; the launch traced here: 33.7 us
  Pallas kernels  33.6 us (99%)
    pallas_call x1, Pallas kernels, gather(): pl.pallas_call(functools.partial(gather_kernel, n_sta, n_tm), out_shape=[...  24.1 us
    pallas_call x1, Pallas kernels, correlate(): pl.pallas_call(functools.partial(correlate_kernel, n_tm), out_shape=jax.S...  9.54 us

profile of v4, /device:TPU:0, one launch (start us, length us, event | category | flops | bytes accessed | tf_op | source)
XLA Modules:
  0.0 33.7 jit_solution(8625709359676398159)
XLA Ops:
  0.0 24.1 %gather_records.1 = (bf16[8,4,128,256]{3,2,1,0:T(8,128)(2,1)}, bf16[3232,1024]{1,0:T(8,128)(2,1)}) custom-call(f32[1,127]{1,0:T(1,128)} %bitcast.3, s32[1,128]{1,0:T(1,128)} %bitcast.5, bf16[128,256]{1,0:T(8,128)(2,1)} %rec_ref.1), custom_call_target="tpu_custom_call" | custom-call | tf_op jit(solution)/shard_map/gather_records/pallas_call | solution.py:243
  24.1 9.5 %correlate_blocks.1 = bf16[3,101,32,128]{3,2,1,0:T(8,128)(2,1)} custom-call(s32[3]{0:T(128)} %plan_ref.1, f32[1,127]{1,0:T(1,128)} %bitcast.4, bf16[8,4,128,256]{3,2,1,0:T(8,128)(2,1)} %get-tuple-element.7.all_ref, bf16[3232,1024]{1,0:T(8,128)(2,1)} %get-tuple-element.8.toep_ref), custom_call_target="tpu_custom_call" | custom-call | tf_op jit(solution)/shard_map/correlate_blocks/pallas_call | solution.py:327

commit v5 on v4

--- a/solution.py
+++ b/solution.py
@@ -50,16 +50,20 @@
         ref[:, EDGE + length:] = blank
 
 
-def normalise(length, coeffs, raw, filt, size, out, out_edge):
+def normalise(length, coeffs, raw, filt, size, rest, out, out_edge):
     band_high, band_low, box = coeffs
     span = TILE + 2 * EDGE
     for t in range(0, length, TILE):
         window = raw[:, t:t + span]
         value = times_rows(window, band_high) + times_rows(window, band_low)
         filt[:, t:t + TILE] = value
-        size[:, EDGE + t:EDGE + t + TILE] = jnp.abs(value).astype(jnp.bfloat16)
+        whole = jnp.abs(value)
+        part = whole.astype(jnp.bfloat16)
+        size[:, EDGE + t:EDGE + t + TILE] = part
+        rest[:, EDGE + t:EDGE + t + TILE] = (whole - part.astype(jnp.float32)).astype(jnp.bfloat16)
     for t in range(0, length, TILE):
-        magnitude = times_rows(size[:, t:t + span], box) * (1.0 / (2 * AVG_HALF + 1)) + 1e-5
+        total = times_rows(size[:, t:t + span], box) + times_rows(rest[:, t:t + span], box)
+        magnitude = total * (1.0 / (2 * AVG_HALF + 1)) + 1e-5
         out[:, out_edge + t:out_edge + t + TILE] = (filt[:, t:t + TILE] / magnitude).astype(jnp.bfloat16)
 
 
@@ -68,9 +72,9 @@
 
 
 def gather_kernel(
-    n_sta, n_tm, taps_ref, valid_ref, rec_ref, all_ref, toep_ref,
-    valid, rec, held, tapline, raw, filt, size, own, toep,
-    in_sem, keep, z_send, z_recv, send, recv, toep_sem,
+    n_sta, n_tm, taps_ref, valid_ref, rec_ref, all_ref, own_ref,
+    taps, valid, rec, held, tapline, raw, filt, size, rest, own,
+    in_sem, keep, z_send, z_recv, send, recv, own_sem,
 ):
     sta = lax.axis_index("sta")
     tm = lax.axis_index("tm")
@@ -88,6 +92,7 @@
     inputs = [
         pltpu.make_async_copy(valid_ref, valid, in_sem.at[0]),
         pltpu.make_async_copy(rec_ref, rec, in_sem.at[1]),
+        pltpu.make_async_copy(taps_ref, taps, in_sem.at[2]),
     ]
     for copy in inputs:
         copy.start()
@@ -109,8 +114,7 @@
 
     own_rows, cols = own.shape[0], rec.shape[1]
     length = n_tm * cols
-    clear_edges(length, raw, size, own)
-    coeffs = bands(taps_ref, tapline)
+    clear_edges(length, raw, size, rest, own)
 
     pl.semaphore_wait(barrier, len(masks) + n_tm - 1)
     started = []
@@ -196,24 +200,6 @@
                 arrival(recv.at[mask, position], mask, position)
                 to_core(mask, position)
 
-    def normalise_own():
-        first = pl.multiple_of(tm * own_rows, own_rows)
-        for c in range(n_tm):
-            raw[:, EDGE + c * cols:EDGE + (c + 1) * cols] = held[0, c, pl.ds(first, own_rows), :]
-        normalise(length, coeffs, raw, filt, size, own, EDGE)
-
-    def lagged_rows(group):
-        l0, count = lag_groups()[group]
-        own_wide = own[...]
-        for l in range(l0, l0 + count):
-            begin = EDGE + (LAGS - 1) // 2 - l
-            toep[l * own_rows:(l + 1) * own_rows, :] = own_wide[:, begin:begin + length]
-        part = pl.ds(l0 * own_rows, count * own_rows)
-        copy = pltpu.make_async_copy(toep.at[part], toep_ref.at[part], toep_sem.at[group])
-        copy.start()
-        kept.append(copy)
-
-    work = [normalise_own] + [functools.partial(lagged_rows, g) for g in range(len(lag_groups()))]
     for turn in range(n_tm + 2):
         if turn < n_tm:
             own_ready(turn)
@@ -221,10 +207,14 @@
             neighbours(turn - 1)
         if turn >= 2:
             far(turn - 2)
-        if turn >= n_tm - 1:
-            work.pop(0)()
-    for step in work:
-        step()
+
+    first = pl.multiple_of(tm * own_rows, own_rows)
+    for c in range(n_tm):
+        raw[:, EDGE + c * cols:EDGE + (c + 1) * cols] = held[0, c, pl.ds(first, own_rows), :]
+    normalise(length, bands(taps, tapline), raw, filt, size, rest, own, EDGE)
+    own_copy = pltpu.make_async_copy(own, own_ref, own_sem)
+    own_copy.start()
+    kept.append(own_copy)
     for position in range(n_tm):
         for mask in range(1, n_sta, 2):
             arrival(recv.at[mask, position], mask, position)
@@ -244,11 +234,12 @@
         functools.partial(gather_kernel, n_sta, n_tm),
         out_shape=[
             jax.ShapeDtypeStruct((n_sta, n_tm, rows, cols), records.dtype),
-            jax.ShapeDtypeStruct((LAGS * own_rows, length), bf16),
+            jax.ShapeDtypeStruct((own_rows, wide), bf16),
         ],
-        in_specs=[pl.BlockSpec(memory_space=pltpu.VMEM)] + [pl.BlockSpec(memory_space=pl.ANY)] * 2,
+        in_specs=[pl.BlockSpec(memory_space=pltpu.HBM)] * 3,
         out_specs=[pl.BlockSpec(memory_space=pl.ANY)] * 2,
         scratch_shapes=[
+            pltpu.VMEM(taps.shape, taps.dtype),
             pltpu.VMEM(valid.shape, valid.dtype),
             pltpu.VMEM((rows, cols), records.dtype),
             pltpu.VMEM((half, n_tm, rows, cols), records.dtype),
@@ -257,26 +248,28 @@
             pltpu.VMEM((own_rows, length), jnp.float32),
             pltpu.VMEM((own_rows, wide), bf16),
             pltpu.VMEM((own_rows, wide), bf16),
-            pltpu.VMEM((LAGS * own_rows, length), bf16),
-            pltpu.SemaphoreType.DMA((2,)),
+            pltpu.VMEM((own_rows, wide), bf16),
+            pltpu.SemaphoreType.DMA((3,)),
             pltpu.SemaphoreType.DMA((half, n_tm)),
             pltpu.SemaphoreType.DMA((n_tm,)),
             pltpu.SemaphoreType.DMA((n_tm,)),
             pltpu.SemaphoreType.DMA((n_sta, n_tm)),
             pltpu.SemaphoreType.DMA((n_sta, n_tm)),
-            pltpu.SemaphoreType.DMA((len(lag_groups()),)),
+            pltpu.SemaphoreType.DMA,
         ],
         compiler_params=pltpu.CompilerParams(
-            collective_id=0, has_side_effects=True, vmem_limit_bytes=60 * 2**20
+            collective_id=0,
+            has_side_effects=True,
+            vmem_limit_bytes=60 * 2**20,
         ),
         name="gather_records",
     )(taps, valid, records)
 
 
-def correlate_kernel(n_tm, plan_ref, taps_ref, all_ref, toep_ref, out_ref, raw, tapline, filt, size, partners, toep, stage, in_sem, toep_sem, out_sem):
+def correlate_kernel(n_tm, plan_ref, taps_ref, all_ref, own_ref, out_ref, taps, own, raw, tapline, filt, size, rest, partners, toep, stage, small_sem, in_sem, out_sem):
     block_rows, cols = all_ref.shape[2], all_ref.shape[3]
     length = n_tm * cols
-    own_rows = toep.shape[0] // LAGS
+    own_rows = own.shape[0]
     sta = lax.axis_index("sta")
     copies = []
     for r in range(ROUNDS):
@@ -286,23 +279,37 @@
                 raw.at[pl.ds(r * block_rows, block_rows), pl.ds(EDGE + c * cols, cols)],
                 in_sem.at[r, c],
             ))
-    toep_copies = []
-    for g, (l0, count) in enumerate(lag_groups()):
-        part = pl.ds(l0 * own_rows, count * own_rows)
-        toep_copies.append(pltpu.make_async_copy(toep_ref.at[part], toep.at[part], toep_sem.at[g]))
-    for copy in copies + toep_copies:
-        copy.start()
-
-    clear_edges(length, raw, size)
-    coeffs = bands(taps_ref, tapline)
+    small = [
+        pltpu.make_async_copy(own_ref, own, small_sem.at[0]),
+        pltpu.make_async_copy(taps_ref, taps, small_sem.at[1]),
+    ]
+    for copy in small + copies:
+        copy.start()
+
+    def lagged_rows(group):
+        l0, count = lag_groups()[group]
+        own_wide = own[...]
+        for l in range(l0, l0 + count):
+            begin = EDGE + (LAGS - 1) // 2 - l
+            toep[l * own_rows:(l + 1) * own_rows, :] = own_wide[:, begin:begin + length]
+
+    groups = len(lag_groups())
+    early = groups // 2
+    clear_edges(length, raw, size, rest)
+    for copy in small:
+        copy.wait()
+    coeffs = bands(taps, tapline)
+    for g in range(early):
+        lagged_rows(g)
     for copy in copies:
         copy.wait()
-    normalise(length, coeffs, raw, filt, size, partners, 0)
+    normalise(length, coeffs, raw, filt, size, rest, partners, 0)
 
     factor = float(length) ** -0.5
     results = []
     for g, (l0, count) in enumerate(lag_groups()):
-        toep_copies[g].wait()
+        if g + early < groups:
+            lagged_rows(g + early)
         rows = toep[l0 * own_rows:(l0 + count) * own_rows, :]
         sums = (times_rows(rows, partners[...]) * factor).astype(jnp.bfloat16)
         for r in range(ROUNDS):
@@ -317,7 +324,7 @@
         result.wait()
 
 
-def correlate(everything, toep, plan, taps):
+def correlate(everything, own, plan, taps):
     n_sta, n_tm, block_rows, cols = everything.shape
     length = n_tm * cols
     own_rows = block_rows // n_tm
@@ -329,33 +336,36 @@
         out_shape=jax.ShapeDtypeStruct((ROUNDS, LAGS, own_rows, block_rows), bf16),
         in_specs=[
             pl.BlockSpec(memory_space=pltpu.SMEM),
-            pl.BlockSpec(memory_space=pltpu.VMEM),
+            pl.BlockSpec(memory_space=pltpu.HBM),
             pl.BlockSpec(memory_space=pl.ANY),
             pl.BlockSpec(memory_space=pl.ANY),
         ],
         out_specs=pl.BlockSpec(memory_space=pl.ANY),
         scratch_shapes=[
+            pltpu.VMEM(taps.shape, taps.dtype),
+            pltpu.VMEM(own.shape, bf16),
             pltpu.VMEM((rows, wide), bf16),
             pltpu.VMEM((8, TILE + 2 * EDGE), jnp.float32),
             pltpu.VMEM((rows, length), jnp.float32),
             pltpu.VMEM((rows, wide), bf16),
+            pltpu.VMEM((rows, wide), bf16),
             pltpu.VMEM((rows, length), bf16),
-            pltpu.VMEM(toep.shape, bf16),
+            pltpu.VMEM((LAGS * own_rows, length), bf16),
             pltpu.VMEM((ROUNDS, LAGS, own_rows, block_rows), bf16),
+            pltpu.SemaphoreType.DMA((2,)),
             pltpu.SemaphoreType.DMA((ROUNDS, n_tm)),
-            pltpu.SemaphoreType.DMA((len(lag_groups()),)),
             pltpu.SemaphoreType.DMA((len(lag_groups()),)),
         ],
         compiler_params=pltpu.CompilerParams(vmem_limit_bytes=60 * 2**20),
         name="correlate_blocks",
-    )(plan, taps, everything, toep)
+    )(plan, taps, everything, own)
 
 
 def local(records, filter_taps, plan, station_valid):
     n_sta, n_tm = lax.axis_size("sta"), lax.axis_size("tm")
     taps = filter_taps[None, :]
-    everything, toep = gather(records, station_valid[None, :], taps, n_sta, n_tm)
-    lagged = correlate(everything, toep, plan, taps)
+    everything, own = gather(records, station_valid[None, :], taps, n_sta, n_tm)
+    lagged = correlate(everything, own, plan, taps)
     return jnp.transpose(lagged, (0, 2, 1, 3))
 
 

time: 33.8 us -> 31.6 us (0.935)
  Pallas kernels: 33.6 us -> 31.4 us
    pallas_call x1, Pallas kernels: 24.1 us -> 21.9 us  [gather(): pl.pallas_call(functools.partial(gather_kernel, n_sta, n_tm), out_shape=[...]
where the time goes in v5:
time: 31.6 us; the launch traced here: 31.4 us
  Pallas kernels  31.4 us (99%)
    pallas_call x1, Pallas kernels, gather(): pl.pallas_call(functools.partial(gather_kernel, n_sta, n_tm), out_shape=[...  21.9 us
    pallas_call x1, Pallas kernels, correlate(): pl.pallas_call(functools.partial(correlate_kernel, n_tm), out_shape=jax.S...  9.41 us

profile of v5, /device:TPU:0, one launch (start us, length us, event | category | flops | bytes accessed | tf_op | source)
XLA Modules:
  0.0 31.4 jit_solution(15639001205530105142)
XLA Ops:
  0.0 21.9 %gather_records.1 = (bf16[8,4,128,256]{3,2,1,0:T(8,128)(2,1)}, bf16[32,1280]{1,0:T(8,128)(2,1)}) custom-call(f32[1,127]{1,0:T(1,128)} %bitcast.3, s32[1,128]{1,0:T(1,128)} %bitcast.5, bf16[128,256]{1,0:T(8,128)(2,1)} %rec_ref.1), custom_call_target="tpu_custom_call" | custom-call | tf_op jit(solution)/shard_map/gather_records/pallas_call | solution.py:233
  22.0 9.4 %correlate_blocks.1 = bf16[3,101,32,128]{3,2,1,0:T(8,128)(2,1)} custom-call(s32[3]{0:T(128)} %plan_ref.1, f32[1,127]{1,0:T(1,128)} %bitcast.4, bf16[8,4,128,256]{3,2,1,0:T(8,128)(2,1)} %get-tuple-element.7.all_ref, bf16[32,1280]{1,0:T(8,128)(2,1)} %get-tuple-element.8.own_ref), custom_call_target="tpu_custom_call" | custom-call | tf_op jit(solution)/shard_map/correlate_blocks/pallas_call | solution.py:334

commit v6 on v3

--- a/solution.py
+++ b/solution.py
@@ -12,7 +12,7 @@
 ROUNDS = 3
 TILE = 256
 EDGE = 128
-LAG_GROUP = 26
+BASE_GROUP = 13
 MESH = pl.DeviceIdType.MESH
 
 
@@ -191,10 +191,18 @@
     return lax.dot_general(left, right, (((1,), (1,)), ((), ())), preferred_element_type=jnp.float32)
 
 
-def correlate_kernel(n_tm, plan_ref, taps_ref, all_ref, out_ref, raw, tapline, filt, high, low, partners, own, toep, stage, in_sem, out_sem):
+def base_groups():
+    half = (LAGS - 1) // 2
+    groups = []
+    for bases in (list(range(half % 2, half + 1, 2)), list(range(half + 1, LAGS, 2))):
+        groups += [bases[i:i + BASE_GROUP] for i in range(0, len(bases), BASE_GROUP)]
+    return groups
+
+
+def correlate_kernel(n_tm, plan_ref, taps_ref, all_ref, out_ref, raw, tapline, filt, high, low, partners, toep, stage, in_sem, out_sem):
     block_rows, cols = all_ref.shape[2], all_ref.shape[3]
     length = n_tm * cols
-    own_rows = own.shape[0]
+    own_rows = block_rows // n_tm
     n_taps = taps_ref.shape[1]
     paired = ROUNDS * block_rows
     sta = lax.axis_index("sta")
@@ -216,7 +224,7 @@
     for copy in copies:
         copy.start()
 
-    for ref in (raw, high, low, own):
+    for ref in (raw, high, low):
         blank = jnp.zeros((ref.shape[0], EDGE), ref.dtype)
         ref[:, :EDGE] = blank
         ref[:, EDGE + length:] = blank
@@ -244,26 +252,41 @@
         total = times_rows(high[:, t:t + span], box) + times_rows(low[:, t:t + span], box)
         magnitude = total * (1.0 / (2 * AVG_HALF + 1)) + 1e-5
         normal = (filt[:, t:t + TILE] / magnitude).astype(jnp.bfloat16)
-        partners[:, t:t + TILE] = normal[:paired]
-        own[:, EDGE + t:EDGE + t + TILE] = normal[paired:]
+        raw[:, EDGE + t:EDGE + t + TILE] = normal
 
     factor = float(length) ** -0.5
     half_lags = (LAGS - 1) // 2
-    own_wide = own[...]
+    own_wide = raw[paired:, :]
+
+    def shifted(place, shift):
+        partners[place * paired:(place + 1) * paired, :] = raw[:paired, EDGE + shift:EDGE + shift + length]
+
+    shifted(0, -1)
+    shifted(1, 0)
     results = []
-    for g, l0 in enumerate(range(0, LAGS, LAG_GROUP)):
-        count = min(LAG_GROUP, LAGS - l0)
-        for l in range(count):
-            begin = EDGE + half_lags - l0 - l
-            toep[(l0 + l) * own_rows:(l0 + l + 1) * own_rows, :] = own_wide[:, begin:begin + length]
-        rows = toep[l0 * own_rows:(l0 + count) * own_rows, :]
-        sums = (times_rows(rows, partners[...]) * factor).astype(jnp.bfloat16)
-        for r in range(ROUNDS):
-            part = sums[:, r * block_rows:(r + 1) * block_rows]
-            stage[r, l0:l0 + count] = part.reshape(count, own_rows, block_rows)
-        result = pltpu.make_async_copy(
-            stage.at[:, pl.ds(l0, count)], out_ref.at[:, pl.ds(l0, count)], out_sem.at[g]
-        )
+    for g, bases in enumerate(base_groups()):
+        before = bases[0] <= half_lags
+        if bases[0] == half_lags + 1:
+            shifted(2, 1)
+        start = 0 if before else paired
+        lags = (-1, 0) if before else (0, 1)
+        top = sum(len(group) for group in base_groups()[:g]) * own_rows
+        for i, l in enumerate(bases):
+            begin = EDGE + half_lags - l
+            toep[top + i * own_rows:top + (i + 1) * own_rows, :] = own_wide[:, begin:begin + length]
+        rows = toep[top:top + len(bases) * own_rows, :]
+        sums = (times_rows(rows, partners[start:start + 2 * paired, :]) * factor).astype(jnp.bfloat16)
+        held_lags = []
+        for i, l in enumerate(bases):
+            for side, extra in enumerate(lags):
+                if not 0 <= l + extra < LAGS:
+                    continue
+                held_lags.append(l + extra)
+                for r in range(ROUNDS):
+                    column = side * paired + r * block_rows
+                    stage[r, l + extra] = sums[i * own_rows:(i + 1) * own_rows, column:column + block_rows]
+        part = pl.ds(min(held_lags), len(held_lags))
+        result = pltpu.make_async_copy(stage.at[:, part], out_ref.at[:, part], out_sem.at[g])
         result.start()
         results.append(result)
     for result in results:
@@ -276,7 +299,7 @@
     own_rows = block_rows // n_tm
     rows = ROUNDS * block_rows + own_rows
     wide = length + 2 * EDGE
-    groups = -(-LAGS // LAG_GROUP)
+    groups = base_groups()
     bf16 = jnp.bfloat16
     return pl.pallas_call(
         functools.partial(correlate_kernel, n_tm),
@@ -293,12 +316,11 @@
             pltpu.VMEM((rows, length), jnp.float32),
             pltpu.VMEM((rows, wide), bf16),
             pltpu.VMEM((rows, wide), bf16),
-            pltpu.VMEM((ROUNDS * block_rows, length), bf16),
-            pltpu.VMEM((own_rows, wide), bf16),
-            pltpu.VMEM((LAGS * own_rows, length), bf16),
+            pltpu.VMEM((3 * ROUNDS * block_rows, length), bf16),
+            pltpu.VMEM((sum(map(len, groups)) * own_rows, length), bf16),
             pltpu.VMEM((ROUNDS, LAGS, own_rows, block_rows), bf16),
             pltpu.SemaphoreType.DMA((ROUNDS + 1, n_tm)),
-            pltpu.SemaphoreType.DMA((groups,)),
+            pltpu.SemaphoreType.DMA((len(groups),)),
         ],
         compiler_params=pltpu.CompilerParams(vmem_limit_bytes=60 * 2**20),
         name="correlate_blocks",

time: 29.8 us -> 29.2 us (0.980)
  Pallas kernels: 29.6 us -> 29 us
    pallas_call x1, Pallas kernels: 8.35 us -> 7.73 us  [correlate(): pl.pallas_call(functools.partial(correlate_kernel, n_tm), out_shape=jax.S...]
where the time goes in v6:
time: 29.2 us; the launch traced here: 29 us
  Pallas kernels  29 us (99%)
    pallas_call x1, Pallas kernels, gather(): pl.pallas_call(functools.partial(gather_kernel, n_sta, n_tm), out_shape=j...  21.3 us
    pallas_call x1, Pallas kernels, correlate(): pl.pallas_call(functools.partial(correlate_kernel, n_tm), out_shape=jax.S...  7.73 us

profile of v6, /device:TPU:0, one launch (start us, length us, event | category | flops | bytes accessed | tf_op | source)
XLA Modules:
  0.0 29.0 jit_solution(323462567237107497)
XLA Ops:
  0.0 21.3 %gather_records.1.all_ref = bf16[8,4,128,256]{3,2,1,0:T(8,128)(2,1)} custom-call(s32[1,128]{1,0:T(1,128)} %bitcast.3, bf16[128,256]{1,0:T(8,128)(2,1)} %rec_ref.1), custom_call_target="tpu_custom_call" | custom-call | tf_op jit(solution)/shard_map/gather_records/pallas_call | solution.py:167
  21.3 7.7 %correlate_blocks.1 = bf16[3,101,32,128]{3,2,1,0:T(8,128)(2,1)} custom-call(s32[3]{0:T(128)} %plan_ref.1, f32[1,127]{1,0:T(1,128)} %bitcast.4, bf16[8,4,128,256]{3,2,1,0:T(8,128)(2,1)} %gather_records.1.all_ref), custom_call_target="tpu_custom_call" | custom-call | tf_op jit(solution)/shard_map/correlate_blocks/pallas_call | solution.py:304

commit v7 on v6

--- a/solution.py
+++ b/solution.py
@@ -206,23 +206,26 @@
     n_taps = taps_ref.shape[1]
     paired = ROUNDS * block_rows
     sta = lax.axis_index("sta")
-    copies = []
-    for r in range(ROUNDS):
-        for c in range(n_tm):
-            copies.append(pltpu.make_async_copy(
+    first = pl.multiple_of(lax.axis_index("tm") * own_rows, own_rows)
+    chunks = []
+    for c in range(n_tm):
+        lanes = pl.ds(EDGE + c * cols, cols)
+        chunks.append([
+            pltpu.make_async_copy(
                 all_ref.at[jnp.bitwise_xor(plan_ref[r], sta), c],
-                raw.at[pl.ds(r * block_rows, block_rows), pl.ds(EDGE + c * cols, cols)],
+                raw.at[pl.ds(r * block_rows, block_rows), lanes],
                 in_sem.at[r, c],
-            ))
-    first = pl.multiple_of(lax.axis_index("tm") * own_rows, own_rows)
-    for c in range(n_tm):
-        copies.append(pltpu.make_async_copy(
-            all_ref.at[sta, c, pl.ds(first, own_rows), :],
-            raw.at[pl.ds(paired, own_rows), pl.ds(EDGE + c * cols, cols)],
-            in_sem.at[ROUNDS, c],
-        ))
-    for copy in copies:
-        copy.start()
+            )
+            for r in range(ROUNDS)
+        ] + [
+            pltpu.make_async_copy(
+                all_ref.at[sta, c, pl.ds(first, own_rows), :],
+                raw.at[pl.ds(paired, own_rows), lanes],
+                in_sem.at[ROUNDS, c],
+            )
+        ])
+        for copy in chunks[c]:
+            copy.start()
 
     for ref in (raw, high, low):
         blank = jnp.zeros((ref.shape[0], EDGE), ref.dtype)
@@ -238,9 +241,12 @@
     ahead = lax.broadcasted_iota(jnp.int32, (TILE, span), 1) - lax.broadcasted_iota(jnp.int32, (TILE, span), 0) - EDGE
     box = jnp.where((ahead >= -AVG_HALF) & (ahead <= AVG_HALF), 1.0, 0.0).astype(jnp.bfloat16)
 
-    for copy in copies:
-        copy.wait()
+    there = 0
     for t in range(0, length, TILE):
+        while there < n_tm and there * cols < t + TILE + EDGE:
+            for copy in chunks[there]:
+                copy.wait()
+            there += 1
         window = raw[:, t:t + span]
         value = times_rows(window, band_high) + times_rows(window, band_low)
         filt[:, t:t + TILE] = value

time: 29.2 us -> 29.8 us (1.021)
  Pallas kernels: 29 us -> 29.6 us
    pallas_call x1, Pallas kernels: 7.73 us -> 8.36 us  [correlate(): pl.pallas_call(functools.partial(correlate_kernel, n_tm), out_shape=jax.S...]
where the time goes in v7:
time: 29.8 us; the launch traced here: 29.6 us
  Pallas kernels  29.6 us (99%)
    pallas_call x1, Pallas kernels, gather(): pl.pallas_call(functools.partial(gather_kernel, n_sta, n_tm), out_shape=j...  21.3 us
    pallas_call x1, Pallas kernels, correlate(): pl.pallas_call(functools.partial(correlate_kernel, n_tm), out_shape=jax.S...  8.36 us

profile of v7, /device:TPU:0, one launch (start us, length us, event | category | flops | bytes accessed | tf_op | source)
XLA Modules:
  0.0 29.6 jit_solution(5353114348632985191)
XLA Ops:
  0.0 21.3 %gather_records.1.all_ref = bf16[8,4,128,256]{3,2,1,0:T(8,128)(2,1)} custom-call(s32[1,128]{1,0:T(1,128)} %bitcast.3, bf16[128,256]{1,0:T(8,128)(2,1)} %rec_ref.1), custom_call_target="tpu_custom_call" | custom-call | tf_op jit(solution)/shard_map/gather_records/pallas_call | solution.py:167
  21.3 8.4 %correlate_blocks.1 = bf16[3,101,32,128]{3,2,1,0:T(8,128)(2,1)} custom-call(s32[3]{0:T(128)} %plan_ref.1, f32[1,127]{1,0:T(1,128)} %bitcast.4, bf16[8,4,128,256]{3,2,1,0:T(8,128)(2,1)} %gather_records.1.all_ref), custom_call_target="tpu_custom_call" | custom-call | tf_op jit(solution)/shard_map/correlate_blocks/pallas_call | solution.py:310

commit v8 on v6

--- a/solution.py
+++ b/solution.py
@@ -263,17 +263,28 @@
 
     shifted(0, -1)
     shifted(1, 0)
+    groups = base_groups()
+
+    def top_of(g):
+        return sum(len(group) for group in groups[:g]) * own_rows
+
+    def build(g):
+        if groups[g][0] == half_lags + 1:
+            shifted(2, 1)
+        for i, l in enumerate(groups[g]):
+            begin = EDGE + half_lags - l
+            row = top_of(g) + i * own_rows
+            toep[row:row + own_rows, :] = own_wide[:, begin:begin + length]
+
     results = []
-    for g, bases in enumerate(base_groups()):
+    build(0)
+    for g, bases in enumerate(groups):
+        if g + 1 < len(groups):
+            build(g + 1)
         before = bases[0] <= half_lags
-        if bases[0] == half_lags + 1:
-            shifted(2, 1)
         start = 0 if before else paired
         lags = (-1, 0) if before else (0, 1)
-        top = sum(len(group) for group in base_groups()[:g]) * own_rows
-        for i, l in enumerate(bases):
-            begin = EDGE + half_lags - l
-            toep[top + i * own_rows:top + (i + 1) * own_rows, :] = own_wide[:, begin:begin + length]
+        top = top_of(g)
         rows = toep[top:top + len(bases) * own_rows, :]
         sums = (times_rows(rows, partners[start:start + 2 * paired, :]) * factor).astype(jnp.bfloat16)
         held_lags = []

time: 29.2 us -> 29.2 us (level)
  no operation moved by 1% of the time
where the time goes in v8:
time: 29.2 us; the launch traced here: 29 us
  Pallas kernels  29 us (99%)
    pallas_call x1, Pallas kernels, gather(): pl.pallas_call(functools.partial(gather_kernel, n_sta, n_tm), out_shape=j...  21.3 us
    pallas_call x1, Pallas kernels, correlate(): pl.pallas_call(functools.partial(correlate_kernel, n_tm), out_shape=jax.S...  7.73 us

profile of v8, /device:TPU:0, one launch (start us, length us, event | category | flops | bytes accessed | tf_op | source)
XLA Modules:
  0.0 29.0 jit_solution(323462567237107497)
XLA Ops:
  0.0 21.3 %gather_records.1.all_ref = bf16[8,4,128,256]{3,2,1,0:T(8,128)(2,1)} custom-call(s32[1,128]{1,0:T(1,128)} %bitcast.3, bf16[128,256]{1,0:T(8,128)(2,1)} %rec_ref.1), custom_call_target="tpu_custom_call" | custom-call | tf_op jit(solution)/shard_map/gather_records/pallas_call | solution.py:167
  21.3 7.7 %correlate_blocks.1 = bf16[3,101,32,128]{3,2,1,0:T(8,128)(2,1)} custom-call(s32[3]{0:T(128)} %plan_ref.1, f32[1,127]{1,0:T(1,128)} %bitcast.4, bf16[8,4,128,256]{3,2,1,0:T(8,128)(2,1)} %gather_records.1.all_ref), custom_call_target="tpu_custom_call" | custom-call | tf_op jit(solution)/shard_map/correlate_blocks/pallas_call | solution.py:315

commit v9 on v6

--- a/solution.py
+++ b/solution.py
@@ -113,7 +113,7 @@
         started.append(copy)
 
     def direct(position):
-        return position == n_tm - 1 or len(outer) != 2
+        return len(outer) != 2
 
     def first_bits(position):
         turn = position % 2

time: 29.2 us -> 30.2 us (1.034)
  Pallas kernels: 29 us -> 30 us
    pallas_call x1, Pallas kernels: 21.3 us -> 22.3 us  [gather(): pl.pallas_call(functools.partial(gather_kernel, n_sta, n_tm), out_shape=j...]
where the time goes in v9:
time: 30.2 us; the launch traced here: 30 us
  Pallas kernels  30 us (99%)
    pallas_call x1, Pallas kernels, gather(): pl.pallas_call(functools.partial(gather_kernel, n_sta, n_tm), out_shape=j...  22.3 us
    pallas_call x1, Pallas kernels, correlate(): pl.pallas_call(functools.partial(correlate_kernel, n_tm), out_shape=jax.S...  7.72 us

profile of v9, /device:TPU:0, one launch (start us, length us, event | category | flops | bytes accessed | tf_op | source)
XLA Modules:
  0.0 30.0 jit_solution(12435149459161844978)
XLA Ops:
  0.0 22.3 %gather_records.1.all_ref = bf16[8,4,128,256]{3,2,1,0:T(8,128)(2,1)} custom-call(s32[1,128]{1,0:T(1,128)} %bitcast.3, bf16[128,256]{1,0:T(8,128)(2,1)} %rec_ref.1), custom_call_target="tpu_custom_call" | custom-call | tf_op jit(solution)/shard_map/gather_records/pallas_call | solution.py:167
  22.3 7.7 %correlate_blocks.1 = bf16[3,101,32,128]{3,2,1,0:T(8,128)(2,1)} custom-call(s32[3]{0:T(128)} %plan_ref.1, f32[1,127]{1,0:T(1,128)} %bitcast.4, bf16[8,4,128,256]{3,2,1,0:T(8,128)(2,1)} %gather_records.1.all_ref), custom_call_target="tpu_custom_call" | custom-call | tf_op jit(solution)/shard_map/correlate_blocks/pallas_call | solution.py:304
